TPU v7x, 32 devices: a whole 2x2x4 slice. The times are simulated.
32 devices in a mesh: hyp: 8 (over y, x, core), head: 4 (over z).
Axes of the slice: x: 2, y: 2, z: 4, core: 2. Of those that a mesh axis runs over, the one named last changes fastest.
Arguments:
- step_embeds: bfloat16 [3, 128, 4096], P(None, 'hyp'), may hold values from -6 to 6
- lang_table: bfloat16 [8, 4096], replicated, may hold values from -3 to 3
- lang_ids: int32 [8, 4], replicated, may hold values from 0 to 7
- self_gain: float32 [4096], replicated, may hold values from 0.1 to 1.9
- self_wq: bfloat16 [4096, 2048], P(None, 'head'), may hold values from -0.09375 to 0.09375
- self_wk: bfloat16 [4096, 2048], P(None, 'head'), may hold values from -0.09375 to 0.09375
- self_wv: bfloat16 [4096, 2048], P(None, 'head'), may hold values from -0.09375 to 0.09375
- self_wo: bfloat16 [2048, 4096], P('head'), may hold values from -0.125 to 0.125
- cross_gain: float32 [4096], replicated, may hold values from 0.1 to 1.9
- cross_wq: bfloat16 [4096, 2048], P(None, 'head'), may hold values from -0.09375 to 0.09375
- cross_wkv: bfloat16 [4096, 4096], P('hyp', 'head'), may hold values from -0.09375 to 0.09375
- encoder_rows: bfloat16 [6144, 4096], P('hyp', 'head'), may hold values from -200 to 200
- doc_lengths: int32 [8], P('hyp'), may hold values from 192 to 768, as said below
- past_keys: bfloat16 [128, 32, 2048], P('hyp', None, 'head'), may hold values from -200 to 200
- past_values: bfloat16 [128, 32, 2048], P('hyp', None, 'head'), may hold values from -6 to 6
- parents: int32 [3, 128], replicated, may hold values from 0 to 3
Outputs:
- cross_context: bfloat16 [3, 128, 2048], P(None, 'hyp', 'head')
- final_keys: bfloat16 [128, 35, 2048], P('hyp', None, 'head')
- final_values: bfloat16 [128, 35, 2048], P('hyp', None, 'head')
Inputs may be any that keep to these rules, and one draw needn't show every extreme that they name: `doc_lengths`: some document has exactly 768 live rows. `parents`: A parent is a beam of the same document and target.
All inputs are finite; a program needn't handle non-finite values.
Results may differ from a plain program's by a relative error of at most 0.03.
Values may be sent and summed in bfloat16 or wider, within the bound.
A program may use at most 128 MiB of HBM per device.

v0:
```python
import jax
import jax.numpy as jnp
from jax import lax
from jax.sharding import PartitionSpec as P

HEAD = 256
BEAMS = 4
TARGETS = 4
STEPS = 3


EPSILON = 1e-06


def shifted(block, axis, distance):
    devices = range(lax.axis_size(axis))
    route = [((i - distance) % len(devices), i) for i in devices]
    return lax.ppermute(block, axis, route)


def rms_scaled(values_in, gain):
    mean_square = jnp.mean(values_in * values_in, axis=-1, keepdims=True)
    return values_in * lax.rsqrt(mean_square + EPSILON) * gain


def pick_rows(candidates, selector, row_axis):
    shape_list = [1] * candidates[0].ndim
    shape_list[row_axis] = selector.shape[0]
    chosen = candidates[0]
    for position in range(1, len(candidates)):
        chosen = jnp.where((selector == position).reshape(shape_list), candidates[position], chosen)
    return chosen


def partial_attend(queries, cache_stack, scaling):
    row_count = cache_stack.shape[1]
    cached = cache_stack.shape[2]
    heads_here = cache_stack.shape[3] // HEAD
    key_part = cache_stack[0].reshape(row_count, cached, heads_here, HEAD)
    value_part = cache_stack[1].reshape(row_count, cached, heads_here, HEAD).astype(jnp.float32)
    scores = (
        jnp.einsum(
            "rhd,rphd->rhp",
            queries.reshape(row_count, heads_here, HEAD),
            key_part,
            preferred_element_type=jnp.float32,
        )
        * scaling
    )
    highest = jnp.max(scores, axis=2)
    raw_weights = jnp.exp(scores - highest[:, :, None])
    totals = jnp.sum(raw_weights, axis=2)
    summed = jnp.einsum("rhp,rphd->rhd", raw_weights, value_part)
    return (highest, totals, summed)


def cross_attend(queries, cross_keys, cross_values, doc_length, scaling):
    query_rows = queries.shape[0]
    heads_here = cross_keys.shape[1]
    scores = (
        jnp.einsum(
            "qhd,jhd->hqj",
            queries.reshape(query_rows, heads_here, HEAD),
            cross_keys,
            preferred_element_type=jnp.float32,
        )
        * scaling
    )
    live_mask = lax.broadcasted_iota(jnp.int32, (1, 1, cross_keys.shape[0]), 2) < doc_length
    scores = jnp.where(live_mask, scores, -jnp.inf)
    highest = jnp.max(scores, axis=2, keepdims=True)
    raw_weights = jnp.exp(scores - highest)
    totals = jnp.sum(raw_weights, axis=2, keepdims=True)
    weights = (raw_weights / totals).astype(jnp.bfloat16)
    output = jnp.einsum("hqj,jhd->qhd", weights, cross_values, preferred_element_type=jnp.float32)
    return output.reshape(query_rows, heads_here * HEAD).astype(jnp.bfloat16)


def shards(
    step_embeds,
    lang_table,
    lang_ids,
    self_gain,
    self_wq,
    self_wk,
    self_wv,
    self_wo,
    cross_gain,
    cross_wq,
    cross_wkv,
    encoder_rows,
    doc_lengths,
    past_keys,
    past_values,
    parents,
):
    hyp_count = lax.axis_size("hyp")
    group_size = hyp_count // BEAMS
    my_index = lax.axis_index("hyp")
    my_beam = my_index // group_size
    my_slot = my_index % group_size
    row_count = step_embeds.shape[1]
    head_width = self_wq.shape[1]
    heads_here = head_width // HEAD
    doc_count = lang_ids.shape[0]
    scaling = HEAD ** (-0.5)
    my_langs = lax.dynamic_slice_in_dim(lang_ids, my_slot * BEAMS, BEAMS, 0).reshape(row_count)
    one_hot = (
        my_langs[:, None] == lax.broadcasted_iota(jnp.int32, (1, lang_table.shape[0]), 1)
    ).astype(jnp.bfloat16)
    lang_rows = jnp.dot(one_hot, lang_table, preferred_element_type=jnp.float32)
    full_weights = lax.all_gather(cross_wkv, "hyp", axis=0, tiled=True)
    cross_kv = jnp.dot(
        lax.all_gather(encoder_rows, "head", axis=1, tiled=True),
        full_weights,
        preferred_element_type=jnp.float32,
    ).astype(jnp.bfloat16)
    cross_kv = cross_kv.reshape(encoder_rows.shape[0], heads_here, 2, HEAD)
    cross_keys = cross_kv[:, :, 0, :]
    cross_values = cross_kv[:, :, 1, :]
    doc_length = doc_lengths[0]
    parent_view = parents.reshape(parents.shape[0], BEAMS, -1)
    my_parents = lax.dynamic_slice_in_dim(parent_view, my_slot * row_count, row_count, 2)
    own_parents = lax.dynamic_index_in_dim(my_parents, my_beam, 1, keepdims=False)
    contexts = []
    cache_stack = jnp.stack([past_keys, past_values])
    for step_idx in range(STEPS):
        offsets = (my_beam - own_parents[step_idx]) % BEAMS
        moved_list = [cache_stack]
        for peer_hop in range(1, BEAMS):
            moved_list.append(shifted(cache_stack, "hyp", peer_hop * group_size))
        cache_stack = pick_rows(moved_list, offsets, 1)
        start_hidden_in = step_embeds[step_idx].astype(jnp.float32) + lang_rows
        normed = rms_scaled(start_hidden_in, self_gain).astype(jnp.bfloat16)
        new_query = jnp.dot(normed, self_wq, preferred_element_type=jnp.float32).astype(
            jnp.bfloat16
        )
        new_key = jnp.dot(normed, self_wk, preferred_element_type=jnp.float32).astype(jnp.bfloat16)
        new_value = jnp.dot(normed, self_wv, preferred_element_type=jnp.float32).astype(
            jnp.bfloat16
        )
        fresh_rows = jnp.stack([new_key, new_value])[:, :, None, :]
        hidden_in, new_query, fresh_rows = (start_hidden_in, new_query, fresh_rows)
        cache_stack = jnp.concatenate([cache_stack, fresh_rows], axis=2)
        attn_parts = partial_attend(new_query, cache_stack, scaling)
        rows_here = hidden_in.shape[0]
        self_context = (
            (attn_parts[2] / attn_parts[1][:, :, None])
            .reshape(rows_here, head_width)
            .astype(jnp.bfloat16)
        )
        partial_out = jnp.dot(self_context, self_wo, preferred_element_type=jnp.float32)
        residual = hidden_in + lax.psum(partial_out.astype(jnp.bfloat16), "head").astype(
            jnp.float32
        )
        normed_cross = rms_scaled(residual, cross_gain).astype(jnp.bfloat16)
        cross_query = jnp.dot(normed_cross, cross_wq, preferred_element_type=jnp.float32).astype(
            jnp.bfloat16
        )
        every_query = lax.all_gather(cross_query, "hyp", axis=0, tiled=True)
        arranged = every_query.reshape(BEAMS, doc_count, TARGETS, head_width)
        doc_queries = lax.dynamic_index_in_dim(arranged, my_index, 1, keepdims=False)
        answer = cross_attend(
            doc_queries.reshape(BEAMS * TARGETS, head_width),
            cross_keys,
            cross_values,
            doc_length,
            scaling,
        )
        every_answer = lax.all_gather(answer, "hyp", axis=0, tiled=True)
        by_owner = every_answer.reshape(doc_count, BEAMS, TARGETS, head_width)
        my_block = lax.dynamic_slice_in_dim(by_owner, my_slot * BEAMS, BEAMS, 0)
        contexts.append(
            lax.dynamic_index_in_dim(my_block, my_beam, 1, keepdims=False).reshape(
                row_count, head_width
            )
        )
    return (jnp.stack(contexts), cache_stack[0], cache_stack[1])


def solution(mesh):
    return jax.shard_map(
        shards,
        mesh=mesh,
        in_specs=(
            P(None, "hyp", None),
            P(),
            P(),
            P(),
            P(None, "head"),
            P(None, "head"),
            P(None, "head"),
            P("head", None),
            P(),
            P(None, "head"),
            P("hyp", "head"),
            P("hyp", "head"),
            P("hyp"),
            P("hyp", None, "head"),
            P("hyp", None, "head"),
            P(),
        ),
        out_specs=(P(None, "hyp", "head"), P("hyp", None, "head"), P("hyp", None, "head")),
        check_vma=False,
    )
```

profile of v0, /device:TPU:0, one launch (start us, length us, event | category | flops | bytes accessed | tf_op | source)
XLA Modules:
  0.0 437.3 jit_solution(3852715313002365695)
XLA Ops:
  10.1 2.9 collective-permute-start.2
  16.9 3.0 fusion.25
  31.2 7.2 %collective-permute-done.2 = bf16[2,16,32,512]{3,1,2,0:T(8,128)(2,1)} collective-permute-done((bf16[2,16,32,512]{3,1,2,0:T(8,128)(2,1)}, bf16[2,16,32,512]{3,1,2,0:T(8,128)(2,1)}, u32[]{:S(2)}, u32[]{:S(2)}) %collective-permute-start.2) | collective-permute-done | bytes 1048608 | tf_op jit(solution)/shard_map/ppermute | solution.py:18
  38.4 21.6 %collective-permute-done.1 = bf16[2,16,32,512]{3,1,2,0:T(8,128)(2,1)} collective-permute-done((bf16[2,16,32,512]{3,1,2,0:T(8,128)(2,1)}, bf16[2,16,32,512]{3,1,2,0:T(8,128)(2,1)}, u32[]{:S(2)}, u32[]{:S(2)}) %collective-permute-start.1) | collective-permute-done | bytes 1048608 | tf_op jit(solution)/shard_map/ppermute | solution.py:18
  68.6 3.5 convolution_convert_fusion.2
  72.1 18.6 %collective-permute-done.3 = bf16[2,16,33,512]{3,1,2,0:T(8,128)(2,1)} collective-permute-done((bf16[2,16,33,512]{3,1,2,0:T(8,128)(2,1)}, bf16[2,16,33,512]{3,1,2,0:T(8,128)(2,1)}, u32[]{:S(2)}, u32[]{:S(2)}) %collective-permute-start.3) | collective-permute-done | bytes 1081376 | tf_op jit(solution)/shard_map/ppermute | solution.py:18
  90.7 23.2 %collective-permute-done.5 = bf16[2,16,33,512]{3,1,2,0:T(8,128)(2,1)} collective-permute-done((bf16[2,16,33,512]{3,1,2,0:T(8,128)(2,1)}, bf16[2,16,33,512]{3,1,2,0:T(8,128)(2,1)}, u32[]{:S(2)}, u32[]{:S(2)}) %collective-permute-start.5) | collective-permute-done | bytes 1081376 | tf_op jit(solution)/shard_map/ppermute | solution.py:18
  124.6 3.5 convolution_convert_fusion.1
  128.1 17.2 %collective-permute-done.6 = bf16[2,16,34,512]{3,1,2,0:T(8,128)(2,1)} collective-permute-done((bf16[2,16,34,512]{3,1,2,0:T(8,128)(2,1)}, bf16[2,16,34,512]{3,1,2,0:T(8,128)(2,1)}, u32[]{:S(2)}, u32[]{:S(2)}) %collective-permute-start.6) | collective-permute-done | bytes 1114144 | tf_op jit(solution)/shard_map/ppermute | solution.py:18
  145.3 22.6 %collective-permute-done.8 = bf16[2,16,34,512]{3,1,2,0:T(8,128)(2,1)} collective-permute-done((bf16[2,16,34,512]{3,1,2,0:T(8,128)(2,1)}, bf16[2,16,34,512]{3,1,2,0:T(8,128)(2,1)}, u32[]{:S(2)}, u32[]{:S(2)}) %collective-permute-start.8) | collective-permute-done | bytes 1114144 | tf_op jit(solution)/shard_map/ppermute | solution.py:18
  172.4 3.5 convolution_convert_fusion
  178.1 35.1 %all-reduce.3.cloned.1.call-done = (bf16[16,4096]{1,0:T(8,128)(2,1)}, bf16[16,4096]{1,0:T(8,128)(2,1)}, bf16[16,4096]{1,0:T(8,128)(2,1)}) async-done(((bf16[16,4096]{1,0:T(8,128)(2,1)}, bf16[16,4096]{1,0:T(8,128)(2,1)}, bf16[16,4096]{1,0:T(8,128)(2,1)}), (bf16[16,4096]{1,0:T(8,128)(2,1)}, bf16[16,4096]{1,0:T(8,128)(2,1)}, bf16[16,4096]{1,0:T(8,128)(2,1)})) %all-reduce.3.cloned.1.call-update) | async-done | bytes 393232 | tf_op jit(solution)/shard_map/psum | solution.py:153
  214.5 3.0 convolution_convert_fusion.11
  217.5 9.1 %all_gather.28 = bf16[128,512]{1,0:T(8,128)(2,1)S(1)} all-gather(bf16[16,512]{1,0:T(8,128)(2,1)S(1)} %convolution_convert_fusion.11), channel_id=1, replica_groups=mesh['hyp'=8,'head'=4] {'hyp'}, dimensions={0}, use_global_device_ids=true | all-gather | bytes 147456 | tf_op jit(solution)/shard_map/all_gather | solution.py:160
  226.7 2.9 convolution_convert_fusion.7
  229.6 9.2 %all_gather.30 = bf16[128,512]{1,0:T(8,128)(2,1)S(1)} all-gather(bf16[16,512]{1,0:T(8,128)(2,1)S(1)} %convolution_convert_fusion.7), channel_id=1, replica_groups=mesh['hyp'=8,'head'=4] {'hyp'}, dimensions={0}, use_global_device_ids=true | all-gather | bytes 147456 | tf_op jit(solution)/shard_map/all_gather | solution.py:160
  241.8 8.4 %all_gather.26 = bf16[128,512]{1,0:T(8,128)(2,1)S(1)} all-gather(bf16[16,512]{1,0:T(8,128)(2,1)S(1)} %convolution_convert_fusion.15), channel_id=1, replica_groups=mesh['hyp'=8,'head'=4] {'hyp'}, dimensions={0}, use_global_device_ids=true | all-gather | bytes 147456 | tf_op jit(solution)/shard_map/all_gather | solution.py:160
  250.3 79.3 %all-gather.3.cloned.1.call-done = bf16[768,4096]{1,0:T(8,128)(2,1)} async-done(((bf16[768,1024]{1,0:T(8,128)(2,1)}), bf16[768,4096]{1,0:T(8,128)(2,1)}) %all-gather.3.cloned.1.call-update) | async-done | bytes 6291472 | tf_op jit(solution)/shard_map/all_gather | solution.py:114
  329.6 54.7 %all-gather.5.cloned.1.call-done = bf16[4096,1024]{1,0:T(8,128)(2,1)} async-done(((bf16[512,1024]{1,0:T(8,128)(2,1)}), bf16[4096,1024]{1,0:T(8,128)(2,1)}) %all-gather.5.cloned.1.call-update) | async-done | bytes 8388624 | tf_op jit(solution)/shard_map/all_gather | solution.py:112
  384.2 10.9 %convolution_convert_fusion.3 = bf16[768,1024]{1,0:T(8,128)(2,1)S(1)} fusion(bf16[768,4096]{1,0:T(8,128)(2,1)} %all-gather.3.cloned.1.call-done, bf16[4096,1024]{1,0:T(8,128)(2,1)} %all-gather.5.cloned.1.call-done), kind=kOutput, calls=%fused_computation.15 | convolution fusion | flops 6443237376 | bytes 16252928 | tf_op jit(solution)/shard_map/dot_general | solution.py:113
  396.4 3.1 fusion.83
  403.3 9.2 %all_gather.31 = bf16[128,512]{1,0:T(8,128)(2,1)S(1)} all-gather(bf16[16,512]{1,0:T(8,128)(2,1)S(1)} %bitcast.234), channel_id=1, replica_groups=mesh['hyp'=8,'head'=4] {'hyp'}, dimensions={0}, use_global_device_ids=true | all-gather | bytes 147456 | tf_op jit(solution)/shard_map/all_gather | solution.py:170
  412.5 8.3 %all_gather.27 = bf16[128,512]{1,0:T(8,128)(2,1)S(1)} all-gather(bf16[16,512]{1,0:T(8,128)(2,1)S(1)} %bitcast.230), channel_id=1, replica_groups=mesh['hyp'=8,'head'=4] {'hyp'}, dimensions={0}, use_global_device_ids=true | all-gather | bytes 147456 | tf_op jit(solution)/shard_map/all_gather | solution.py:170
  420.9 9.2 %all_gather.29 = bf16[128,512]{1,0:T(8,128)(2,1)S(1)} all-gather(bf16[16,512]{1,0:T(8,128)(2,1)S(1)} %bitcast.229), channel_id=1, replica_groups=mesh['hyp'=8,'head'=4] {'hyp'}, dimensions={0}, use_global_device_ids=true | all-gather | bytes 147456 | tf_op jit(solution)/shard_map/all_gather | solution.py:170
  (142 shorter events, 53.5 us)
Async XLA Ops:
  7.2 9.1 %copy-start = (bf16[8,4096]{1,0:T(8,128)(2,1)S(1)}, bf16[8,4096]{1,0:T(8,128)(2,1)}, u32[]{:S(2)}) copy-start(bf16[8,4096]{1,0:T(8,128)(2,1)} %param.17) | copy-start | bytes 196612
  7.2 206.0 %all-reduce.3.cloned.1.call-start = ((), (), s32[]{:S(2)}) async-start(), calls=%async_computation.2 | async-start | bytes 786432 | tf_op jit(solution)/shard_map/psum | solution.py:153
  9.0 7.0 %copy-start.13 = (s32[8,4]{0,1:T(4,128)S(1)}, s32[8,4]{0,1:T(4,128)}, u32[]{:S(2)}) copy-start(s32[8,4]{0,1:T(4,128)} %param.18) | copy-start | bytes 388
  9.0 7.3 %copy-start.5 = (bf16[3,16,4096]{2,1,0:T(8,128)(2,1)S(1)}, bf16[3,16,4096]{2,1,0:T(8,128)(2,1)}, u32[]{:S(2)}) copy-start(bf16[3,16,4096]{2,1,0:T(8,128)(2,1)} %param.16) | copy-start | bytes 1179652
  9.0 7.7 %copy-start.12 = (f32[4096]{0:T(1024)S(1)}, f32[4096]{0:T(1024)}, u32[]{:S(2)}) copy-start(f32[4096]{0:T(1024)} %param.19) | copy-start | bytes 49156
  10.1 28.2 %collective-permute-start.2 = (bf16[2,16,32,512]{3,1,2,0:T(8,128)(2,1)}, bf16[2,16,32,512]{3,1,2,0:T(8,128)(2,1)}, u32[]{:S(2)}, u32[]{:S(2)}) collective-permute-start(bf16[2,16,32,512]{3,1,2,0:T(8,128)(2,1)} %pad_maximum_fusion.2), channel_id=1, source_target_pairs={{24,0},{28,4},{0,8},{4,12},{8,16},{12,20},{16,24},{20,28},{25,1},{... | collective-permute-start | bytes 3145736 | tf_op jit(solution)/shard_map/ppermute | solution.py:18
  13.1 46.9 %collective-permute-start.1 = (bf16[2,16,32,512]{3,1,2,0:T(8,128)(2,1)}, bf16[2,16,32,512]{3,1,2,0:T(8,128)(2,1)}, u32[]{:S(2)}, u32[]{:S(2)}) collective-permute-start(bf16[2,16,32,512]{3,1,2,0:T(8,128)(2,1)} %pad_maximum_fusion.2), channel_id=1, source_target_pairs={{16,0},{20,4},{24,8},{28,12},{0,16},{4,20},{8,24},{12,28},{17,1},{... | collective-permute-start | bytes 3145736 | tf_op jit(solution)/shard_map/ppermute | solution.py:18
  14.6 45.7 %collective-permute-start = (bf16[2,16,32,512]{3,1,2,0:T(8,128)(2,1)}, bf16[2,16,32,512]{3,1,2,0:T(8,128)(2,1)}, u32[]{:S(2)}, u32[]{:S(2)}) collective-permute-start(bf16[2,16,32,512]{3,1,2,0:T(8,128)(2,1)} %pad_maximum_fusion.2), channel_id=1, source_target_pairs={{8,0},{12,4},{16,8},{20,12},{24,16},{28,20},{0,24},{4,28},{9,1},{1... | collective-permute-start | bytes 3145736 | tf_op jit(solution)/shard_map/ppermute | solution.py:18
  16.9 3.5 copy-start.4
  20.4 2.2 copy-start.2
  23.2 2.2 copy-start.3
  63.6 27.1 %collective-permute-start.3 = (bf16[2,16,33,512]{3,1,2,0:T(8,128)(2,1)}, bf16[2,16,33,512]{3,1,2,0:T(8,128)(2,1)}, u32[]{:S(2)}, u32[]{:S(2)}) collective-permute-start(bf16[2,16,33,512]{3,1,2,0:T(8,128)(2,1)} %pad_maximum_fusion.1), channel_id=1, source_target_pairs={{8,0},{12,4},{16,8},{20,12},{24,16},{28,20},{0,24},{4,28},{9,1},{1... | collective-permute-start | bytes 3244040 | tf_op jit(solution)/shard_map/ppermute | solution.py:18
  65.1 48.8 %collective-permute-start.5 = (bf16[2,16,33,512]{3,1,2,0:T(8,128)(2,1)}, bf16[2,16,33,512]{3,1,2,0:T(8,128)(2,1)}, u32[]{:S(2)}, u32[]{:S(2)}) collective-permute-start(bf16[2,16,33,512]{3,1,2,0:T(8,128)(2,1)} %pad_maximum_fusion.1), channel_id=1, source_target_pairs={{24,0},{28,4},{0,8},{4,12},{8,16},{12,20},{16,24},{20,28},{25,1},{... | collective-permute-start | bytes 3244040 | tf_op jit(solution)/shard_map/ppermute | solution.py:18
  65.6 48.4 %collective-permute-start.4 = (bf16[2,16,33,512]{3,1,2,0:T(8,128)(2,1)}, bf16[2,16,33,512]{3,1,2,0:T(8,128)(2,1)}, u32[]{:S(2)}, u32[]{:S(2)}) collective-permute-start(bf16[2,16,33,512]{3,1,2,0:T(8,128)(2,1)} %pad_maximum_fusion.1), channel_id=1, source_target_pairs={{16,0},{20,4},{24,8},{28,12},{0,16},{4,20},{8,24},{12,28},{17,1},{... | collective-permute-start | bytes 3244040 | tf_op jit(solution)/shard_map/ppermute | solution.py:18
  117.4 27.9 %collective-permute-start.6 = (bf16[2,16,34,512]{3,1,2,0:T(8,128)(2,1)}, bf16[2,16,34,512]{3,1,2,0:T(8,128)(2,1)}, u32[]{:S(2)}, u32[]{:S(2)}) collective-permute-start(bf16[2,16,34,512]{3,1,2,0:T(8,128)(2,1)} %pad_maximum_fusion), channel_id=1, source_target_pairs={{8,0},{12,4},{16,8},{20,12},{24,16},{28,20},{0,24},{4,28},{9,1},{1... | collective-permute-start | bytes 3342344 | tf_op jit(solution)/shard_map/ppermute | solution.py:18
  117.6 50.2 %collective-permute-start.8 = (bf16[2,16,34,512]{3,1,2,0:T(8,128)(2,1)}, bf16[2,16,34,512]{3,1,2,0:T(8,128)(2,1)}, u32[]{:S(2)}, u32[]{:S(2)}) collective-permute-start(bf16[2,16,34,512]{3,1,2,0:T(8,128)(2,1)} %pad_maximum_fusion), channel_id=1, source_target_pairs={{24,0},{28,4},{0,8},{4,12},{8,16},{12,20},{16,24},{20,28},{25,1},{... | collective-permute-start | bytes 3342344 | tf_op jit(solution)/shard_map/ppermute | solution.py:18
  119.5 49.0 %collective-permute-start.7 = (bf16[2,16,34,512]{3,1,2,0:T(8,128)(2,1)}, bf16[2,16,34,512]{3,1,2,0:T(8,128)(2,1)}, u32[]{:S(2)}, u32[]{:S(2)}) collective-permute-start(bf16[2,16,34,512]{3,1,2,0:T(8,128)(2,1)} %pad_maximum_fusion), channel_id=1, source_target_pairs={{16,0},{20,4},{24,8},{28,12},{0,16},{4,20},{8,24},{12,28},{17,1},{... | collective-permute-start | bytes 3342344 | tf_op jit(solution)/shard_map/ppermute | solution.py:18
  175.9 38.6 %copy-start.11 = (f32[4096]{0:T(1024)S(1)}, f32[4096]{0:T(1024)}, u32[]{:S(2)}) copy-start(f32[4096]{0:T(1024)} %param.24) | copy-start | bytes 49156
  175.9 153.7 %all-gather.3.cloned.1.call-start = ((), (), s32[]{:S(2)}) async-start(), calls=%async_computation | async-start | bytes 7864320 | tf_op jit(solution)/shard_map/all_gather | solution.py:114
  176.7 207.6 %all-gather.5.cloned.1.call-start = ((), (), s32[]{:S(2)}) async-start(), calls=%async_computation.1 | async-start | bytes 9437184 | tf_op jit(solution)/shard_map/all_gather | solution.py:112
  214.5 12.2 %copy-start.10 = (bf16[16,4096]{1,0:T(8,128)(2,1)S(1)}, bf16[16,4096]{1,0:T(8,128)(2,1)}, u32[]{:S(2)}) copy-start(bf16[16,4096]{1,0:T(8,128)(2,1)} %get-tuple-element.9) | copy-start | bytes 393220
  226.7 12.2 %copy-start.9 = (bf16[16,4096]{1,0:T(8,128)(2,1)S(1)}, bf16[16,4096]{1,0:T(8,128)(2,1)}, u32[]{:S(2)}) copy-start(bf16[16,4096]{1,0:T(8,128)(2,1)} %get-tuple-element.10) | copy-start | bytes 393220
  399.4 2.3 copy-start.8
  402.7 28.0 %copy-start.1 = (bf16[8,4096]{1,0:T(8,128)(2,1)S(1)}, bf16[8,4096]{1,0:T(8,128)(2,1)}, u32[]{:S(2)}) copy-start(bf16[8,4096]{1,0:T(8,128)(2,1)} %param.17) | copy-start | bytes 196612
  (3 other events, 3.7 us)
Sparse Core Ops, SparseCore 0:
  176.0 37.0 all-reduce.2
  214.8 114.7 all-gather.2
  331.6 52.5 all-gather.4
where the time goes:
time: 438 us; the launch traced here: 437 us
  waiting for transfers between devices  282 us (64%)
  blocking collectives  53.3 us (12%)
  matrix products  48.6 us (11%)
  between operations  14.9 us (3%)
  starting transfers between devices  13.5 us (3%)
  other arithmetic  13 us (3%)
  local copies, waits for them, and re-layouts  12.4 us (3%)
    ppermute x9, waiting for transfers between devices, shifted(): return lax.ppermute(block, axis, route)  111 us
    all_gather x1, waiting for transfers between devices, shards(): lax.all_gather(encoder_rows, 'head', axis=1, tiled=True)  79.3 us
    all_gather x1, waiting for transfers between devices, shards(): full_weights = lax.all_gather(cross_wkv, 'hyp', axis=0, tiled=True)  54.7 us
    psum x1, waiting for transfers between devices, shards(): lax.psum(partial_out.astype(jnp.bfloat16), 'head').astype(jnp.float32)  35.1 us
    all_gather x3, blocking collectives, shards(): every_query = lax.all_gather(cross_query, 'hyp', axis=0, tiled=True)  26.7 us
    all_gather x3, blocking collectives, shards(): every_answer = lax.all_gather(answer, 'hyp', axis=0, tiled=True)  26.6 us
    ppermute x9, starting transfers between devices, shifted(): return lax.ppermute(block, axis, route)  13.2 us
    dot_general x1, matrix products, shards(): jnp.dot(lax.all_gather(encoder_rows, 'head', axis=1, tiled=True), full_we...  10.9 us
  transfers between devices with their start and end apart: 12, of which 12 were waited for; matrix products, arithmetic and copies ran while one was open for 8% of the time, Pallas kernels for 0%

commit v1 on v0

v1 whole, which is shorter than its diff:
```python
import jax
import jax.numpy as jnp
from jax import lax
from jax.sharding import PartitionSpec as P

HEAD = 256
BEAMS = 4
STEPS = 3
EPSILON = 1e-06


def rms_scaled(values_in, gain):
    mean_square = jnp.mean(values_in * values_in, axis=-1, keepdims=True)
    return values_in * lax.rsqrt(mean_square + EPSILON) * gain


def pick(candidates, selector):
    chosen = candidates[0]
    shape = selector.shape + (1,) * (chosen.ndim - selector.ndim)
    for position in range(1, len(candidates)):
        chosen = jnp.where((selector == position).reshape(shape), candidates[position], chosen)
    return chosen


def choose(flags, first, second):
    return jnp.where(flags.reshape(flags.shape + (1,) * (first.ndim - flags.ndim)), first, second)


def compose(outer, inner):
    return pick([jnp.broadcast_to(outer[b][None], inner.shape) for b in range(BEAMS)], inner)


def swap(block, bit, group_size):
    count = lax.axis_size("hyp")
    route = [(i, ((i // group_size) ^ bit) * group_size + i % group_size) for i in range(count)]
    return lax.ppermute(block, "hyp", route)


def final_cache(past, bit, my_beam, ancestors, group_size):
    other = 3 - bit
    mate = swap(past, bit, group_size)
    mine_set = (my_beam & bit) != 0
    low = jnp.where(mine_set, mate, past)
    high = jnp.where(mine_set, past, mate)
    peer_rows = lax.dynamic_index_in_dim(ancestors, my_beam ^ other, 0, keepdims=False)
    my_rows = lax.dynamic_index_in_dim(ancestors, my_beam, 0, keepdims=False)
    arrived = swap(choose((peer_rows & bit) != 0, high, low), other, group_size)
    local = choose((my_rows & bit) != 0, high, low)
    return choose((my_rows & other) == (my_beam & other), local, arrived)


def cross_attend(queries, cross_keys, cross_values, doc_length):
    query_rows = queries.shape[0]
    heads_here = cross_keys.shape[1]
    scores = jnp.einsum(
        "qhd,jhd->hqj",
        queries.reshape(query_rows, heads_here, HEAD),
        cross_keys,
        preferred_element_type=jnp.float32,
    ) * (HEAD ** (-0.5))
    live_mask = lax.broadcasted_iota(jnp.int32, (1, 1, cross_keys.shape[0]), 2) < doc_length
    scores = jnp.where(live_mask, scores, -jnp.inf)
    highest = jnp.max(scores, axis=2, keepdims=True)
    raw_weights = jnp.exp(scores - highest)
    totals = jnp.sum(raw_weights, axis=2, keepdims=True)
    weights = (raw_weights / totals).astype(jnp.bfloat16)
    output = jnp.einsum("hqj,jhd->qhd", weights, cross_values, preferred_element_type=jnp.float32)
    return output.reshape(query_rows, heads_here * HEAD).astype(jnp.bfloat16)


def project_rows(encoder_rows, cross_wkv):
    size = lax.axis_size("head")
    me = lax.axis_index("head")
    width = encoder_rows.shape[1]
    full_weights = lax.all_gather(cross_wkv, "hyp", axis=0, tiled=True)

    def term(rows, owner):
        owner = jnp.clip(owner, 0, size - 1)
        weights = lax.dynamic_slice_in_dim(full_weights, owner * width, width, 0)
        return jnp.dot(rows, weights, preferred_element_type=jnp.float32)

    upward = [(i, i + 1) for i in range(size - 1)]
    downward = [(i + 1, i) for i in range(size - 1)]
    up = down = encoder_rows
    total = term(encoder_rows, me)
    for step in range(1, size):
        up = lax.ppermute(up, "head", upward)
        down = lax.ppermute(down, "head", downward)
        total = total + term(up, me - step)
        total = total + term(down, me + step)
        upward, downward = upward[1:], downward[:-1]
    return total.astype(jnp.bfloat16)


def shards(
    step_embeds,
    lang_table,
    lang_ids,
    self_gain,
    self_wq,
    self_wk,
    self_wv,
    self_wo,
    cross_gain,
    cross_wq,
    cross_wkv,
    encoder_rows,
    doc_lengths,
    past_keys,
    past_values,
    parents,
):
    hyp_count = lax.axis_size("hyp")
    head_parts = lax.axis_size("head")
    group_size = hyp_count // BEAMS
    my_index = lax.axis_index("hyp")
    my_beam = my_index // group_size
    my_slot = my_index % group_size
    rows = step_embeds.shape[1]
    features = step_embeds.shape[2]
    head_width = self_wq.shape[1]
    heads = head_width // HEAD
    past = past_keys.shape[1]
    docs_here = lang_ids.shape[0] // group_size
    targets = lang_ids.shape[1]
    scaling = HEAD ** (-0.5)
    beam_groups = [[b * group_size + s for b in range(BEAMS)] for s in range(group_size)]

    cross_kv = project_rows(encoder_rows, cross_wkv)
    cross_kv = cross_kv.reshape(encoder_rows.shape[0], heads, 2, HEAD)

    my_langs = lax.dynamic_slice_in_dim(lang_ids, my_slot * docs_here, docs_here, 0).reshape(rows)
    one_hot = (
        my_langs[:, None] == lax.broadcasted_iota(jnp.int32, (1, lang_table.shape[0]), 1)
    ).astype(jnp.bfloat16)
    lang_rows = jnp.dot(one_hot, lang_table, preferred_element_type=jnp.float32)
    hidden_in = (step_embeds.astype(jnp.float32) + lang_rows[None]).reshape(STEPS * rows, features)
    normed = rms_scaled(hidden_in, self_gain).astype(jnp.bfloat16)
    made = [
        jnp.dot(normed, w, preferred_element_type=jnp.float32).astype(jnp.bfloat16)
        for w in (self_wq, self_wk, self_wv)
    ]
    every = lax.all_gather(
        jnp.concatenate(made, axis=1), "hyp", axis=0, tiled=False, axis_index_groups=beam_groups
    ).reshape(BEAMS, STEPS, rows, 3, head_width)
    queries, keys, values = every[:, :, :, 0], every[:, :, :, 1], every[:, :, :, 2]

    parent_view = parents.reshape(STEPS, BEAMS, -1)
    moves = lax.dynamic_slice_in_dim(parent_view, my_slot * rows, rows, 2)
    ancestors = []
    for s in range(STEPS):
        chain = {s: None}
        current = moves[s]
        for j in range(s - 1, -2, -1):
            chain[j] = current
            if j >= 0:
                current = compose(moves[j], current)
        ancestors.append(chain)

    def of_mine(table):
        return lax.dynamic_index_in_dim(table, my_beam, 0, keepdims=False)

    past_k = past_keys.reshape(rows, past, heads, HEAD)
    past_v = past_values.reshape(rows, past, heads, HEAD)
    split_q = queries.reshape(BEAMS * STEPS, rows, heads, HEAD)
    scores = (
        jnp.einsum("nrhd,rphd->rhnp", split_q, past_k, preferred_element_type=jnp.float32)
        * scaling
    )
    highest = jnp.max(scores, axis=3)
    weights = jnp.exp(scores - highest[..., None])
    totals = jnp.sum(weights, axis=3)
    summed = jnp.einsum("rhnp,rphd->nrhd", weights, past_v.astype(jnp.float32))
    stats = jnp.stack([highest, totals], axis=-1).transpose(2, 0, 1, 3)
    packed = jnp.concatenate(
        [
            summed.reshape(BEAMS, STEPS * rows, head_width),
            stats.reshape(BEAMS, STEPS * rows, heads * 2),
        ],
        axis=2,
    )
    returned = lax.all_to_all(
        packed, "hyp", 0, 0, tiled=True, axis_index_groups=beam_groups
    ).reshape(BEAMS, STEPS, rows, head_width + heads * 2)
    past_of = jnp.stack([of_mine(ancestors[s][-1]) for s in range(STEPS)])
    chosen = pick([returned[b] for b in range(BEAMS)], past_of)
    part_sum = chosen[..., :head_width].reshape(STEPS, rows, heads, HEAD)
    part_stats = chosen[..., head_width:].reshape(STEPS, rows, heads, 2)

    contexts = []
    last_keys, last_values = [], []
    for s in range(STEPS):
        my_query = of_mine(queries[:, s]).reshape(rows, heads, HEAD).astype(jnp.float32)
        high, added, score_list, value_list = part_stats[s, ..., 0], None, [], []
        for j in range(s + 1):
            if j == s:
                key, value = of_mine(keys[:, j]), of_mine(values[:, j])
            else:
                owner = of_mine(ancestors[s][j])
                key = pick([keys[b, j] for b in range(BEAMS)], owner)
                value = pick([values[b, j] for b in range(BEAMS)], owner)
            if s == STEPS - 1:
                last_keys.append(key)
                last_values.append(value)
            key = key.reshape(rows, heads, HEAD).astype(jnp.float32)
            score_list.append(jnp.sum(my_query * key, axis=-1) * scaling)
            value_list.append(value.reshape(rows, heads, HEAD).astype(jnp.float32))
        top = high
        for score in score_list:
            top = jnp.maximum(top, score)
        factor = jnp.exp(high - top)
        total = part_stats[s, ..., 1] * factor
        context = part_sum[s] * factor[..., None]
        for score, value in zip(score_list, value_list):
            weight = jnp.exp(score - top)
            total = total + weight
            context = context + weight[..., None] * value
        contexts.append((context / total[..., None]).reshape(rows, head_width))
    self_context = jnp.concatenate(contexts, axis=0).astype(jnp.bfloat16)

    partial_out = jnp.dot(self_context, self_wo, preferred_element_type=jnp.float32).astype(
        jnp.bfloat16
    )
    share = features // head_parts
    spread = lax.all_to_all(
        partial_out.reshape(STEPS * rows, head_parts, share).transpose(1, 0, 2),
        "head", 0, 0, tiled=True,
    )
    own_sum = jnp.sum(spread.astype(jnp.float32), axis=0).astype(jnp.bfloat16)
    full_sum = lax.all_gather(own_sum, "head", axis=1, tiled=True)
    residual = hidden_in + full_sum.astype(jnp.float32)
    normed_cross = rms_scaled(residual, cross_gain).astype(jnp.bfloat16)
    cross_query = jnp.dot(normed_cross, cross_wq, preferred_element_type=jnp.float32).astype(
        jnp.bfloat16
    )

    by_doc = cross_query.reshape(STEPS, docs_here, targets, head_width).transpose(1, 0, 2, 3)
    by_doc = by_doc.reshape(1, docs_here, STEPS * targets, head_width)
    slots = jnp.arange(group_size)
    outgoing = jnp.where(
        (slots == my_slot)[:, None, None, None], by_doc, jnp.zeros((), by_doc.dtype)
    ).reshape(hyp_count, STEPS * targets, head_width)
    incoming = lax.all_to_all(outgoing, "hyp", 0, 0, tiled=True)
    source_slot = my_index // docs_here
    doc_queries = lax.dynamic_index_in_dim(
        incoming.reshape(BEAMS, group_size, STEPS * targets, head_width), source_slot, 1, False
    ).reshape(BEAMS * STEPS * targets, head_width)
    answer = cross_attend(doc_queries, cross_kv[:, :, 0, :], cross_kv[:, :, 1, :], doc_lengths[0])

    by_beam = answer.reshape(BEAMS, 1, STEPS * targets, head_width)
    outgoing = jnp.where(
        (slots == source_slot)[None, :, None, None], by_beam, jnp.zeros((), by_beam.dtype)
    ).reshape(hyp_count, STEPS * targets, head_width)
    incoming = lax.all_to_all(outgoing, "hyp", 0, 0, tiled=True)
    mine = lax.dynamic_slice_in_dim(incoming, my_slot * docs_here, docs_here, 0)
    cross_context = (
        mine.reshape(docs_here, STEPS, targets, head_width)
        .transpose(1, 0, 2, 3)
        .reshape(STEPS, rows, head_width)
    )

    last = ancestors[STEPS - 1][-1]
    out_keys = final_cache(past_keys, 1, my_beam, last, group_size)
    out_values = final_cache(past_values, 2, my_beam, last, group_size)
    final_keys = jnp.concatenate([out_keys, jnp.stack(last_keys, axis=1)], axis=1)
    final_values = jnp.concatenate([out_values, jnp.stack(last_values, axis=1)], axis=1)
    return (cross_context, final_keys, final_values)


def solution(mesh):
    return jax.shard_map(
        shards,
        mesh=mesh,
        in_specs=(
            P(None, "hyp", None),
            P(),
            P(),
            P(),
            P(None, "head"),
            P(None, "head"),
            P(None, "head"),
            P("head", None),
            P(),
            P(None, "head"),
            P("hyp", "head"),
            P("hyp", "head"),
            P("hyp"),
            P("hyp", None, "head"),
            P("hyp", None, "head"),
            P(),
        ),
        out_specs=(P(None, "hyp", "head"), P("hyp", None, "head"), P("hyp", None, "head")),
        check_vma=False,
    )
```

time: 438 us -> 213 us (0.49)
  waiting for transfers between devices: 282 us -> 43.5 us
  blocking collectives: 53.3 us -> 28.9 us
  starting transfers between devices: 13.5 us -> 33.4 us
  local copies, waits for them, and re-layouts: 12.4 us -> 31.2 us
  matrix products: 48.6 us -> 37.2 us
  other arithmetic: 13 us -> 21.6 us
    all_gather x2 -> x1, waiting for transfers between devices: 134 us -> 0.02 us  [project_rows(): full_weights = lax.all_gather(cross_wkv, 'hyp', axis=0, tiled=True)]
    ppermute x9 -> x10, waiting for transfers between devices: 111 us -> 25.8 us  [the longest x3 25.8 us: project_rows(): down = lax.ppermute(down, 'head', downward)]
    psum x1 -> x0, waiting for transfers between devices: 35.1 us -> none  [shards(): lax.psum(partial_out.astype(jnp.bfloat16), 'head').astype(jnp.float32)]
    all_gather x6 -> x2, blocking collectives: 53.3 us -> 28.9 us  [the longest x1 15.2 us: shards(): full_sum = lax.all_gather(own_sum, 'head', axis=1, tiled=True)]
    all_to_all x0 -> x4, waiting for transfers between devices: none -> 16.9 us  [the longest x2 9.86 us: shards(): incoming = lax.all_to_all(outgoing, 'hyp', 0, 0, tiled=True)]
    all_to_all x0 -> x4, starting transfers between devices: none -> 15.6 us  [the longest x2 6.74 us: shards(): incoming = lax.all_to_all(outgoing, 'hyp', 0, 0, tiled=True)]
    dot_general x3 -> x1, matrix products: 10.5 us -> 3.06 us  [shards(): jnp.dot(self_context, self_wo, preferred_element_type=jnp.float32)]
    dot_general x3 -> x1, matrix products: 8.81 us -> 3.02 us  [shards(): jnp.dot(normed_cross, cross_wq, preferred_element_type=jnp.float32)]
  transfers between devices with their start and end apart: 12 -> 15, of which waited for: 12 -> 5; matrix products, arithmetic and copies ran while one was open for 8% -> 38% of each run, Pallas kernels for 0% -> 0%
where the time goes in v1:
time: 213 us; the launch traced here: 211 us
  waiting for transfers between devices  43.5 us (20%)
  matrix products  37.2 us (17%)
  starting transfers between devices  33.4 us (16%)
  local copies, waits for them, and re-layouts  31.2 us (15%)
  blocking collectives  28.9 us (14%)
  other arithmetic  21.6 us (10%)
  between operations  15.8 us (7%)
    ppermute x3, waiting for transfers between devices, project_rows(): down = lax.ppermute(down, 'head', downward)  25.8 us
    dot_general x7, matrix products, term(): return jnp.dot(rows, weights, preferred_element_type=jnp.float32)  23.9 us
    all_gather x1, blocking collectives, shards(): full_sum = lax.all_gather(own_sum, 'head', axis=1, tiled=True)  15.2 us
    all_gather x1, blocking collectives, shards(): lax.all_gather(jnp.concatenate(made, axis=1), 'hyp', axis=0, tiled=False,...  13.7 us
    all_to_all x2, waiting for transfers between devices, shards(): incoming = lax.all_to_all(outgoing, 'hyp', 0, 0, tiled=True)  9.86 us
    ppermute x3, starting transfers between devices, project_rows(): up = lax.ppermute(up, 'head', upward)  9.77 us
    unnamed x79, local copies, waits for them, and re-layouts  7.19 us
    all_to_all x1, waiting for transfers between devices, shards(): lax.all_to_all(partial_out.reshape(STEPS * rows, head_parts, share).trans...  7.06 us
  transfers between devices with their start and end apart: 15, of which 5 were waited for; matrix products, arithmetic and copies ran while one was open for 38% of the time, Pallas kernels for 0%

profile of v1, /device:TPU:0, one launch (start us, length us, event | category | flops | bytes accessed | tf_op | source)
XLA Modules:
  0.0 211.5 jit_solution(13683779809167804572)
XLA Ops:
  7.9 6.1 %collective-permute-start = (bf16[768,1024]{1,0:T(8,128)(2,1)}, bf16[768,1024]{1,0:T(8,128)(2,1)}, u32[]{:S(2)}, u32[]{:S(2)}) collective-permute-start(bf16[768,1024]{1,0:T(8,128)(2,1)} %param.27), channel_id=1, source_target_pairs={{0,1},{1,2},{2,3},{4,5},{5,6},{6,7},{8,9},{9,10},{10,11},{12,13},{... | collective-permute-start | bytes 4718600 | tf_op jit(solution)/shard_map/ppermute | solution.py:87
  18.8 4.0 %convolution_convert_fusion.3 = bf16[48,512]{1,0:T(8,128)(2,1)S(1)} fusion(bf16[48,4096]{1,0:T(8,128)(2,1)S(1)} %fusion.22, bf16[4096,512]{1,0:T(8,128)(2,1)} %param.22), kind=kOutput, calls=%fused_computation.25 | convolution fusion | flops 201351168 | bytes 4636672 | tf_op jit(solution)/shard_map/dot_general | solution.py:140
  25.9 13.7 %all-gather = bf16[192,1536]{1,0:T(8,128)(2,1)S(1)} all-gather(bf16[48,1536]{1,0:T(8,128)(2,1)S(1)} %pad_maximum_fusion.3), channel_id=2, replica_groups={{0,8,16,24},{4,12,20,28},{1,9,17,25},{5,13,21,29},{2,10,18,26},{6,14,22..., dimensions={0}, use_global_device_ids=true | all-gather | bytes 737280 | tf_op jit(solution)/shard_map/all_gather | solution.py:143
  40.1 2.4 %fusion.89 = (bf16[4,3,16,1,512]{4,3,2,1,0:T(2,128)(2,1)}, bf16[4,3,16,512]{3,2,1,0:T(8,128)(2,1)S(1)}, bf16[4,3,16,1,512]{4,3,2,1,0:T(2,128)(2,1)}, bf16[4,3,16,1,512]{4,3,2,1,0:T(2,128)(2,1)S(1)}) fusion(bf16[4,3,16,3,512]{4,3,2,1,0:T(4,128)(2,1)S(1)} %reshape.1120), kind=kLoop, calls=%fused_computation.224 | loop fusion | bytes 1376256 | tf_op jit(solution)/shard_map/slice | solution.py:146
  45.4 4.1 %all-to-all-start = ((f32[4,48,516]{2,1,0:T(8,128)}), f32[4,48,516]{2,1,0:T(8,128)}, u32[]{:S(2)}, u32[]{:S(2)}) async-start(f32[4,48,516]{2,1,0:T(8,128)} %pad_maximum_fusion.2), calls=%async_computation | async-start | bytes 983040 | tf_op jit(solution)/shard_map/all_to_all | solution.py:182
  50.6 2.0 collective-permute-start.6
  86.0 3.1 %convolution_convert_fusion = bf16[48,4096]{1,0:T(8,128)(2,1)S(1)} fusion(bf16[512,4096]{1,0:T(8,128)(2,1)} %param.23, bf16[16,512]{1,0:T(8,128)(2,1)S(1)} %fusion.51, bf16[16,512]{1,0:T(8,128)(2,1)S(1)} %get-tuple-element.58, bf16[16,512]{1,0:T(8,128)(2,1)S(1)} %get-tuple-element.57), kind=kOutput, calls=%fused_computation.1 | convolution fusion | flops 201670656 | bytes 4636672 | tf_op jit(solution)/shard_map/dot_general | solution.py:221
  89.9 4.7 %all-to-all-start.1 = ((bf16[4,48,1024]{2,1,0:T(8,128)(2,1)}), bf16[4,48,1024]{2,1,0:T(8,128)(2,1)S(1)}, u32[]{:S(2)}, u32[]{:S(2)}) async-start(bf16[4,48,1024]{2,1,0:T(8,128)(2,1)} %bitcast.357), calls=%async_computation.1 | async-start | bytes 786432 | tf_op jit(solution)/shard_map/all_to_all | solution.py:225
  97.4 7.1 %all-to-all-done.1 = bf16[4,48,1024]{2,1,0:T(8,128)(2,1)S(1)} async-done(((bf16[4,48,1024]{2,1,0:T(8,128)(2,1)}), bf16[4,48,1024]{2,1,0:T(8,128)(2,1)S(1)}, u32[]{:S(2)}, u32[]{:S(2)}) %all-to-all-start.1) | async-done | bytes 393248 | tf_op jit(solution)/shard_map/all_to_all | solution.py:225
  104.5 15.2 %all_gather.15 = bf16[48,4096]{1,0:T(8,128)(2,1)S(1)} all-gather(bf16[48,1024]{1,0:T(8,128)(2,1)S(1)} %reduce_sum.110), channel_id=1, replica_groups=mesh['hyp'=8,'head'=4] {'head'}, dimensions={1}, use_global_device_ids=true | all-gather | bytes 491520 | tf_op jit(solution)/shard_map/all_gather | solution.py:230
  123.2 3.0 %convolution_convert_fusion.2 = bf16[48,512]{1,0:T(8,128)(2,1)S(1)} fusion(bf16[48,4096]{1,0:T(8,128)(2,1)S(1)} %multiply_convert_fusion, bf16[4096,512]{1,0:T(8,128)(2,1)} %param.25), kind=kOutput, calls=%fused_computation.24 | convolution fusion | flops 201351168 | bytes 4636672 | tf_op jit(solution)/shard_map/dot_general | solution.py:233
  127.1 3.4 %all-to-all-start.2 = ((bf16[8,12,512]{2,1,0:T(8,128)(2,1)}), bf16[8,12,512]{2,1,0:T(8,128)(2,1)S(1)}, u32[]{:S(2)}, u32[]{:S(2)}) async-start(bf16[8,12,512]{2,1,0:T(8,128)(2,1)} %bitcast_select_fusion.1), calls=%async_computation.2 | async-start | bytes 262144 | tf_op jit(solution)/shard_map/all_to_all | solution.py:243
  130.6 5.3 %all-to-all-done.2 = bf16[8,12,512]{2,1,0:T(8,128)(2,1)S(1)} async-done(((bf16[8,12,512]{2,1,0:T(8,128)(2,1)}), bf16[8,12,512]{2,1,0:T(8,128)(2,1)S(1)}, u32[]{:S(2)}, u32[]{:S(2)}) %all-to-all-start.2) | async-done | bytes 98336 | tf_op jit(solution)/shard_map/all_to_all | solution.py:243
  141.6 15.2 %collective-permute-done.3 = bf16[768,1024]{1,0:T(8,128)(2,1)} collective-permute-done((bf16[768,1024]{1,0:T(8,128)(2,1)}, bf16[768,1024]{1,0:T(8,128)(2,1)}, u32[]{:S(2)}, u32[]{:S(2)}) %collective-permute-start.3) | collective-permute-done | bytes 1572896 | tf_op jit(solution)/shard_map/ppermute | solution.py:88
  158.3 4.0 %fusion.5 = f32[1024,768]{1,0:T(8,128)S(1)} fusion(bf16[768,1024]{1,0:T(8,128)(2,1)} %collective-permute-done.3, bf16[4096,1024]{1,0:T(8,128)(2,1)} %all-gather.3.cloned.1.call-done, s32[]{:T(128)S(6)} %select_n.397), kind=kOutput, calls=%fused_computation.7 | convolution fusion | flops 1610612736 | bytes 6815748 | tf_op jit(solution)/shard_map/dot_general | solution.py:80
  162.8 3.3 %fusion.7 = f32[1024,768]{1,0:T(8,128)S(1)} fusion(bf16[768,1024]{1,0:T(8,128)(2,1)} %collective-permute-done.2, bf16[4096,1024]{1,0:T(8,128)(2,1)S(1)} %copy-done.6, s32[]{:T(128)S(6)} %select_n.396), kind=kOutput, calls=%fused_computation.9 | convolution fusion | flops 1610612736 | bytes 6815748 | tf_op jit(solution)/shard_map/dot_general | solution.py:80
  166.1 3.4 %fusion.9 = f32[1024,768]{1,0:T(8,128)S(1)} fusion(bf16[768,1024]{1,0:T(8,128)(2,1)} %collective-permute-done.1, bf16[4096,1024]{1,0:T(8,128)(2,1)S(1)} %copy-done.6, s32[]{:T(128)S(6)} %select_n.395), kind=kOutput, calls=%fused_computation.11 | convolution fusion | flops 1610612736 | bytes 6815748 | tf_op jit(solution)/shard_map/dot_general | solution.py:80
  169.5 1.9 fusion.13
  171.4 3.3 %fusion.11 = f32[1024,768]{1,0:T(8,128)S(1)} fusion(bf16[768,1024]{1,0:T(8,128)(2,1)} %collective-permute-done, bf16[4096,1024]{1,0:T(8,128)(2,1)S(1)} %copy-done.6, s32[]{:T(128)S(6)} %select_n.394), kind=kOutput, calls=%fused_computation.13 | convolution fusion | flops 1610612736 | bytes 6815748 | tf_op jit(solution)/shard_map/dot_general | solution.py:80
  174.7 3.3 %fusion.3 = f32[1024,768]{1,0:T(8,128)S(1)} fusion(bf16[768,1024]{1,0:T(8,128)(2,1)} %collective-permute-done.4, bf16[4096,1024]{1,0:T(8,128)(2,1)S(1)} %copy-done.6, s32[]{:T(128)S(6)} %select_n.398), kind=kOutput, calls=%fused_computation.5 | convolution fusion | flops 1610612736 | bytes 6815748 | tf_op jit(solution)/shard_map/dot_general | solution.py:80
  178.0 10.7 %collective-permute-done.5 = bf16[768,1024]{1,0:T(8,128)(2,1)} collective-permute-done((bf16[768,1024]{1,0:T(8,128)(2,1)}, bf16[768,1024]{1,0:T(8,128)(2,1)}, u32[]{:S(2)}, u32[]{:S(2)}) %collective-permute-start.5) | collective-permute-done | bytes 1572896 | tf_op jit(solution)/shard_map/ppermute | solution.py:88
  188.6 4.8 %add_convert_fusion = bf16[1024,768]{1,0:T(8,128)(2,1)S(1)} fusion(f32[1024,768]{1,0:T(8,128)S(1)} %fusion.3, f32[1024,768]{1,0:T(8,128)S(1)} %fusion.5, f32[1024,768]{1,0:T(8,128)S(1)} %fusion.7, f32[1024,768]{1,0:T(8,128)S(1)} %fusion.9, f32[1024,768]{1,0:T(8,128)S(1)} %fusion.13, f32[1024,768]{1,0:T(8,128)S(1)} %fusion.11, ...), kind=kOutput, calls=%fused_computation.2 | convolution fusion | flops 1616117760 | bytes 24117252 | tf_op jit(solution)/shard_map/dot_general | solution.py:80
  195.1 3.4 %all-to-all-start.3 = ((bf16[8,12,512]{2,1,0:T(8,128)(2,1)}), bf16[8,12,512]{2,1,0:T(8,128)(2,1)S(1)}, u32[]{:S(2)}, u32[]{:S(2)}) async-start(bf16[8,12,512]{2,1,0:T(8,128)(2,1)} %bitcast_select_fusion), calls=%async_computation.3 | async-start | bytes 262144 | tf_op jit(solution)/shard_map/all_to_all | solution.py:254
  199.4 4.5 %all-to-all-done.3 = bf16[8,12,512]{2,1,0:T(8,128)(2,1)S(1)} async-done(((bf16[8,12,512]{2,1,0:T(8,128)(2,1)}), bf16[8,12,512]{2,1,0:T(8,128)(2,1)S(1)}, u32[]{:S(2)}, u32[]{:S(2)}) %all-to-all-start.3) | async-done | bytes 98336 | tf_op jit(solution)/shard_map/all_to_all | solution.py:254
  (233 shorter events, 63.9 us)
Async XLA Ops:
  7.2 151.1 %all-gather.3.cloned.1.call-start = ((), (), s32[]{:S(2)}) async-start(), calls=%async_computation.4 | async-start | bytes 9437184 | tf_op jit(solution)/shard_map/all_gather | solution.py:75
  7.9 112.0 %collective-permute-start = (bf16[768,1024]{1,0:T(8,128)(2,1)}, bf16[768,1024]{1,0:T(8,128)(2,1)}, u32[]{:S(2)}, u32[]{:S(2)}) collective-permute-start(bf16[768,1024]{1,0:T(8,128)(2,1)} %param.27), channel_id=1, source_target_pairs={{0,1},{1,2},{2,3},{4,5},{5,6},{6,7},{8,9},{9,10},{10,11},{12,13},{... | collective-permute-start | bytes 4718600 | tf_op jit(solution)/shard_map/ppermute | solution.py:87
  14.0 107.7 %collective-permute-start.1 = (bf16[768,1024]{1,0:T(8,128)(2,1)}, bf16[768,1024]{1,0:T(8,128)(2,1)}, u32[]{:S(2)}, u32[]{:S(2)}) collective-permute-start(bf16[768,1024]{1,0:T(8,128)(2,1)} %param.27), channel_id=1, source_target_pairs={{1,0},{2,1},{3,2},{5,4},{6,5},{7,6},{9,8},{10,9},{11,10},{13,12},{... | collective-permute-start | bytes 4718600 | tf_op jit(solution)/shard_map/ppermute | solution.py:88
  25.9 16.7 %copy-start.3 = (bf16[16,32,512]{2,1,0:T(8,128)(2,1)S(1)}, bf16[16,32,512]{2,1,0:T(8,128)(2,1)}, u32[]{:S(2)}) copy-start(bf16[16,32,512]{2,1,0:T(8,128)(2,1)} %param.29) | copy-start | bytes 1572868
  45.4 28.8 %all-to-all-start = ((f32[4,48,516]{2,1,0:T(8,128)}), f32[4,48,516]{2,1,0:T(8,128)}, u32[]{:S(2)}, u32[]{:S(2)}) async-start(f32[4,48,516]{2,1,0:T(8,128)} %pad_maximum_fusion.2), calls=%async_computation | async-start | bytes 983040 | tf_op jit(solution)/shard_map/all_to_all | solution.py:182
  50.6 44.0 %collective-permute-start.6 = (bf16[16,32,512]{2,0,1:T(8,128)(2,1)}, bf16[16,32,512]{2,0,1:T(8,128)(2,1)S(1)}, u32[]{:S(2)}, u32[]{:S(2)}) collective-permute-start(bf16[16,32,512]{2,0,1:T(8,128)(2,1)} %copy.259), channel_id=1, source_target_pairs={{0,8},{4,12},{8,0},{12,4},{16,24},{20,28},{24,16},{28,20},{1,9},{5... | collective-permute-start | bytes 1572872 | tf_op jit(solution)/shard_map/ppermute | solution.py:36
  53.7 42.6 %collective-permute-start.8 = (bf16[16,32,512]{2,0,1:T(8,128)(2,1)}, bf16[16,32,512]{2,0,1:T(8,128)(2,1)S(1)}, u32[]{:S(2)}, u32[]{:S(2)}) collective-permute-start(bf16[16,32,512]{2,0,1:T(8,128)(2,1)} %copy.262), channel_id=1, source_target_pairs={{0,16},{4,20},{8,24},{12,28},{16,0},{20,4},{24,8},{28,12},{1,17},{... | collective-permute-start | bytes 1572872 | tf_op jit(solution)/shard_map/ppermute | solution.py:36
  63.4 13.9 %copy-start.13 = (pred[16]{0:T(512)(128)(4,1)}, pred[16]{0:T(512)(128)(4,1)S(1)}, u32[]{:S(2)}) copy-start(pred[16]{0:T(512)(128)(4,1)S(1)} %get-tuple-element.85) | copy-start | bytes 52
  63.5 14.0 %copy-start.20 = (pred[16]{0:T(512)(128)(4,1)}, pred[16]{0:T(512)(128)(4,1)S(1)}, u32[]{:S(2)}) copy-start(pred[16]{0:T(512)(128)(4,1)S(1)} %get-tuple-element.102) | copy-start | bytes 52
  63.5 14.0 %copy-start.21 = (pred[16]{0:T(512)(128)(4,1)}, pred[16]{0:T(512)(128)(4,1)S(1)}, u32[]{:S(2)}) copy-start(pred[16]{0:T(512)(128)(4,1)S(1)} %get-tuple-element.103) | copy-start | bytes 52
  89.9 33.2 %copy-start.12 = (f32[4096]{0:T(1024)S(1)}, f32[4096]{0:T(1024)}, u32[]{:S(2)}) copy-start(f32[4096]{0:T(1024)} %param.24) | copy-start | bytes 49156
  89.9 14.6 %all-to-all-start.1 = ((bf16[4,48,1024]{2,1,0:T(8,128)(2,1)}), bf16[4,48,1024]{2,1,0:T(8,128)(2,1)S(1)}, u32[]{:S(2)}, u32[]{:S(2)}) async-start(bf16[4,48,1024]{2,1,0:T(8,128)(2,1)} %bitcast.357), calls=%async_computation.1 | async-start | bytes 786432 | tf_op jit(solution)/shard_map/all_to_all | solution.py:225
  95.8 40.2 %collective-permute-start.7 = (bf16[16,32,512]{2,0,1:T(8,128)(2,1)}, bf16[16,32,512]{2,0,1:T(8,128)(2,1)}, u32[]{:S(2)}, u32[]{:S(2)}) collective-permute-start(bf16[16,32,512]{2,0,1:T(8,128)(2,1)} %broadcast_select_fusion.1), channel_id=1, source_target_pairs={{0,16},{4,20},{8,24},{12,28},{16,0},{20,4},{24,8},{28,12},{1,17},{... | collective-permute-start | bytes 1572872 | tf_op jit(solution)/shard_map/ppermute | solution.py:36
  97.4 41.0 %collective-permute-start.9 = (bf16[16,32,512]{2,0,1:T(8,128)(2,1)}, bf16[16,32,512]{2,0,1:T(8,128)(2,1)}, u32[]{:S(2)}, u32[]{:S(2)}) collective-permute-start(bf16[16,32,512]{2,0,1:T(8,128)(2,1)} %broadcast_select_fusion), channel_id=1, source_target_pairs={{0,8},{4,12},{8,0},{12,4},{16,24},{20,28},{24,16},{28,20},{1,9},{5... | collective-permute-start | bytes 1572872 | tf_op jit(solution)/shard_map/ppermute | solution.py:36
  119.9 19.9 %collective-permute-start.2 = (bf16[768,1024]{1,0:T(8,128)(2,1)}, bf16[768,1024]{1,0:T(8,128)(2,1)}, u32[]{:S(2)}, u32[]{:S(2)}) collective-permute-start(bf16[768,1024]{1,0:T(8,128)(2,1)} %collective-permute-done), channel_id=1, source_target_pairs={{1,2},{2,3},{5,6},{6,7},{9,10},{10,11},{13,14},{14,15},{17,18},{18... | collective-permute-start | bytes 4718600 | tf_op jit(solution)/shard_map/ppermute | solution.py:87
  121.7 35.0 %collective-permute-start.3 = (bf16[768,1024]{1,0:T(8,128)(2,1)}, bf16[768,1024]{1,0:T(8,128)(2,1)}, u32[]{:S(2)}, u32[]{:S(2)}) collective-permute-start(bf16[768,1024]{1,0:T(8,128)(2,1)} %collective-permute-done.1), channel_id=1, source_target_pairs={{1,0},{2,1},{5,4},{6,5},{9,8},{10,9},{13,12},{14,13},{17,16},{18,1... | collective-permute-start | bytes 4718600 | tf_op jit(solution)/shard_map/ppermute | solution.py:88
  123.2 14.2 %copy-start.7 = (bf16[16,1,512]{2,0,1:T(8,128)(2,1)S(1)}, bf16[16,1,512]{2,0,1:T(8,128)(2,1)}, u32[]{:S(2)}) copy-start(bf16[16,1,512]{2,0,1:T(8,128)(2,1)} %get-tuple-element.59) | copy-start | bytes 49156
  123.2 14.2 %copy-start.10 = (bf16[16,1,512]{2,0,1:T(8,128)(2,1)S(1)}, bf16[16,1,512]{2,0,1:T(8,128)(2,1)}, u32[]{:S(2)}) copy-start(bf16[16,1,512]{2,0,1:T(8,128)(2,1)} %get-tuple-element.38) | copy-start | bytes 49156
  123.2 14.2 %copy-start.11 = (bf16[16,1,512]{2,0,1:T(8,128)(2,1)S(1)}, bf16[16,1,512]{2,0,1:T(8,128)(2,1)}, u32[]{:S(2)}) copy-start(bf16[16,1,512]{2,0,1:T(8,128)(2,1)} %get-tuple-element.39) | copy-start | bytes 49156
  127.1 8.8 %all-to-all-start.2 = ((bf16[8,12,512]{2,1,0:T(8,128)(2,1)}), bf16[8,12,512]{2,1,0:T(8,128)(2,1)S(1)}, u32[]{:S(2)}, u32[]{:S(2)}) async-start(bf16[8,12,512]{2,1,0:T(8,128)(2,1)} %bitcast_select_fusion.1), calls=%async_computation.2 | async-start | bytes 262144 | tf_op jit(solution)/shard_map/all_to_all | solution.py:243
  139.8 34.9 %collective-permute-start.4 = (bf16[768,1024]{1,0:T(8,128)(2,1)}, bf16[768,1024]{1,0:T(8,128)(2,1)}, u32[]{:S(2)}, u32[]{:S(2)}) collective-permute-start(bf16[768,1024]{1,0:T(8,128)(2,1)} %collective-permute-done.2), channel_id=1, source_target_pairs={{2,3},{6,7},{10,11},{14,15},{18,19},{22,23},{26,27},{30,31}} | collective-permute-start | bytes 4718600 | tf_op jit(solution)/shard_map/ppermute | solution.py:87
  156.8 31.8 %collective-permute-start.5 = (bf16[768,1024]{1,0:T(8,128)(2,1)}, bf16[768,1024]{1,0:T(8,128)(2,1)}, u32[]{:S(2)}, u32[]{:S(2)}) collective-permute-start(bf16[768,1024]{1,0:T(8,128)(2,1)} %collective-permute-done.3), channel_id=1, source_target_pairs={{1,0},{5,4},{9,8},{13,12},{17,16},{21,20},{25,24},{29,28}} | collective-permute-start | bytes 4718600 | tf_op jit(solution)/shard_map/ppermute | solution.py:88
  188.6 16.0 %copy-start.1 = (bf16[8,4096]{1,0:T(8,128)(2,1)S(1)}, bf16[8,4096]{1,0:T(8,128)(2,1)}, u32[]{:S(2)}) copy-start(bf16[8,4096]{1,0:T(8,128)(2,1)} %param.17) | copy-start | bytes 196612
  195.1 8.8 %all-to-all-start.3 = ((bf16[8,12,512]{2,1,0:T(8,128)(2,1)}), bf16[8,12,512]{2,1,0:T(8,128)(2,1)S(1)}, u32[]{:S(2)}, u32[]{:S(2)}) async-start(bf16[8,12,512]{2,1,0:T(8,128)(2,1)} %bitcast_select_fusion), calls=%async_computation.3 | async-start | bytes 262144 | tf_op jit(solution)/shard_map/all_to_all | solution.py:254
  (22 other events, 209.2 us)
Sparse Core Ops, SparseCore 0:
  9.9 75.8 all-gather.2

commit v2 on v1

--- a/solution.py
+++ b/solution.py
@@ -1,6 +1,10 @@
+import functools
+
 import jax
 import jax.numpy as jnp
 from jax import lax
+from jax.experimental import pallas as pl
+from jax.experimental.pallas import tpu as pltpu
 from jax.sharding import PartitionSpec as P
 
 HEAD = 256
@@ -49,47 +53,206 @@
     return choose((my_rows & other) == (my_beam & other), local, arrived)
 
 
-def cross_attend(queries, cross_keys, cross_values, doc_length):
-    query_rows = queries.shape[0]
-    heads_here = cross_keys.shape[1]
-    scores = jnp.einsum(
-        "qhd,jhd->hqj",
-        queries.reshape(query_rows, heads_here, HEAD),
-        cross_keys,
-        preferred_element_type=jnp.float32,
-    ) * (HEAD ** (-0.5))
-    live_mask = lax.broadcasted_iota(jnp.int32, (1, 1, cross_keys.shape[0]), 2) < doc_length
-    scores = jnp.where(live_mask, scores, -jnp.inf)
-    highest = jnp.max(scores, axis=2, keepdims=True)
-    raw_weights = jnp.exp(scores - highest)
-    totals = jnp.sum(raw_weights, axis=2, keepdims=True)
-    weights = (raw_weights / totals).astype(jnp.bfloat16)
-    output = jnp.einsum("hqj,jhd->qhd", weights, cross_values, preferred_element_type=jnp.float32)
-    return output.reshape(query_rows, heads_here * HEAD).astype(jnp.bfloat16)
+def cross_attend(queries, cross_kv, doc_length):
+    rows = cross_kv.shape[0]
+    live_mask = lax.broadcasted_iota(jnp.int32, (1, rows), 1) < doc_length
+    outputs = []
+    for head in range(queries.shape[1] // HEAD):
+        query = queries[:, head * HEAD : (head + 1) * HEAD]
+        keys = cross_kv[:, 2 * head * HEAD : (2 * head + 1) * HEAD]
+        values = cross_kv[:, (2 * head + 1) * HEAD : (2 * head + 2) * HEAD]
+        scores = lax.dot_general(
+            query, keys, (((1,), (1,)), ((), ())), preferred_element_type=jnp.float32
+        ) * (HEAD ** (-0.5))
+        scores = jnp.where(live_mask, scores, -jnp.inf)
+        raw_weights = jnp.exp(scores - jnp.max(scores, axis=1, keepdims=True))
+        totals = jnp.sum(raw_weights, axis=1, keepdims=True)
+        weights = (raw_weights / totals).astype(jnp.bfloat16)
+        outputs.append(jnp.dot(weights, values, preferred_element_type=jnp.float32))
+    return jnp.concatenate(outputs, axis=1).astype(jnp.bfloat16)
+
+
+def gather_weights(block):
+    size = lax.axis_size("hyp")
+    me = lax.axis_index("hyp")
+    blocks = block[None]
+    bits = [1 << k for k in range(1, size.bit_length() - 1)] + [1]
+    done = 0
+    for bit in bits:
+        arrived = lax.ppermute(blocks, "hyp", [(i, i ^ bit) for i in range(size)])
+        mine_high = (me & bit) != 0
+        low = jnp.where(mine_high, arrived, blocks)
+        high = jnp.where(mine_high, blocks, arrived)
+        if bit > done:
+            blocks = jnp.concatenate([low, high], axis=0)
+        else:
+            blocks = jnp.stack([low, high], axis=1).reshape((-1,) + block.shape)
+        done = max(done, bit)
+    return blocks.reshape(size * block.shape[0], block.shape[1])
 
 
 def project_rows(encoder_rows, cross_wkv):
+    half = encoder_rows.shape[0] // 2
+    parts = [
+        lax.all_gather(encoder_rows[k * half : (k + 1) * half], "head", axis=1, tiled=True)
+        for k in range(2)
+    ]
+    full_weights = gather_weights(cross_wkv)
+    return jnp.concatenate(
+        [
+            jnp.dot(part, full_weights, preferred_element_type=jnp.float32).astype(jnp.bfloat16)
+            for part in parts
+        ],
+        axis=0,
+    )
+
+
+def cross_query_kernel(
+    docs_here, context, wo, hidden, gain, wq, arrived,
+    part, landed, full, query, sum_send, sum_recv, all_send, all_recv, out_send, out_recv,
+):
     size = lax.axis_size("head")
     me = lax.axis_index("head")
-    width = encoder_rows.shape[1]
-    full_weights = lax.all_gather(cross_wkv, "hyp", axis=0, tiled=True)
-
-    def term(rows, owner):
-        owner = jnp.clip(owner, 0, size - 1)
-        weights = lax.dynamic_slice_in_dim(full_weights, owner * width, width, 0)
-        return jnp.dot(rows, weights, preferred_element_type=jnp.float32)
-
-    upward = [(i, i + 1) for i in range(size - 1)]
-    downward = [(i + 1, i) for i in range(size - 1)]
-    up = down = encoder_rows
-    total = term(encoder_rows, me)
-    for step in range(1, size):
-        up = lax.ppermute(up, "head", upward)
-        down = lax.ppermute(down, "head", downward)
-        total = total + term(up, me - step)
-        total = total + term(down, me + step)
-        upward, downward = upward[1:], downward[:-1]
-    return total.astype(jnp.bfloat16)
+    hyps = lax.axis_size("hyp")
+    group = hyps // BEAMS
+    index = lax.axis_index("hyp")
+    slot = lax.rem(index, group)
+    beam = index // group
+    share = part.shape[2]
+    targets = [slot * docs_here + k for k in range(docs_here)]
+    sources = [b * group + index // docs_here for b in range(BEAMS)]
+
+    barrier = pltpu.get_barrier_semaphore()
+    for d in range(1, size):
+        pl.semaphore_signal(
+            barrier, 1, device_id=(index, lax.rem(me + d, size)), device_id_type=pl.DeviceIdType.MESH
+        )
+    expected = jnp.int32(size - 1)
+    for peer in targets + sources:
+        expected = expected + (peer != index).astype(jnp.int32)
+
+        @pl.when(peer != index)
+        def _():
+            pl.semaphore_signal(
+                barrier, 1, device_id=(peer, me), device_id_type=pl.DeviceIdType.MESH
+            )
+
+    for c in range(size):
+        part[c] = jnp.dot(
+            context[...], wo[:, c * share : (c + 1) * share], preferred_element_type=jnp.float32
+        ).astype(jnp.bfloat16)
+    pl.semaphore_wait(barrier, expected)
+
+    def spread(d):
+        peer = lax.rem(me + d, size)
+        return pltpu.make_async_remote_copy(
+            part.at[peer], landed.at[d - 1], sum_send.at[d - 1], sum_recv.at[d - 1],
+            device_id=(index, peer), device_id_type=pl.DeviceIdType.MESH,
+        )
+
+    def share_out(d):
+        peer = lax.rem(me + d, size)
+        return pltpu.make_async_remote_copy(
+            full.at[me], full.at[me], all_send.at[d - 1], all_recv.at[d - 1],
+            device_id=(index, peer), device_id_type=pl.DeviceIdType.MESH,
+        )
+
+    def share_in(d):
+        source = lax.rem(me + size - d, size)
+        return pltpu.make_async_remote_copy(
+            full.at[source], full.at[source], all_send.at[d - 1], all_recv.at[d - 1],
+            device_id=(index, source), device_id_type=pl.DeviceIdType.MESH,
+        )
+
+    for d in range(1, size):
+        spread(d).start()
+    total = part[me].astype(jnp.float32)
+    for d in range(1, size):
+        spread(d).wait_recv()
+        total = total + landed[d - 1].astype(jnp.float32)
+    full[me] = total.astype(jnp.bfloat16)
+    for d in range(1, size):
+        share_out(d).start()
+    for d in range(1, size):
+        share_in(d).wait_recv()
+
+    square = jnp.zeros((hidden.shape[0], 1), jnp.float32)
+    for c in range(size):
+        residual = hidden[:, c * share : (c + 1) * share] + full[c].astype(jnp.float32)
+        square = square + jnp.sum(residual * residual, axis=1, keepdims=True)
+    factor = lax.rsqrt(square / hidden.shape[1] + EPSILON)
+    answer = jnp.zeros(query.shape, jnp.float32)
+    for c in range(size):
+        columns = slice(c * share, (c + 1) * share)
+        residual = hidden[:, columns] + full[c].astype(jnp.float32)
+        normed = (residual * factor * gain[:, columns]).astype(jnp.bfloat16)
+        answer = answer + jnp.dot(normed, wq[columns, :], preferred_element_type=jnp.float32)
+    query[...] = answer.astype(jnp.bfloat16)
+
+    def send_query(k):
+        return pltpu.make_async_remote_copy(
+            query, arrived.at[beam], out_send.at[k], out_recv.at[beam],
+            device_id=(targets[k], me), device_id_type=pl.DeviceIdType.MESH,
+        )
+
+    for k in range(docs_here):
+
+        @pl.when(targets[k] != index)
+        def _(k=k):
+            send_query(k).start()
+
+        @pl.when(targets[k] == index)
+        def _():
+            arrived[beam] = query[...]
+
+    for b in range(BEAMS):
+
+        @pl.when(sources[b] != index)
+        def _(b=b):
+            pltpu.make_async_remote_copy(
+                query, arrived.at[b], out_send.at[0], out_recv.at[b],
+                device_id=(sources[b], me), device_id_type=pl.DeviceIdType.MESH,
+            ).wait_recv()
+
+    for d in range(1, size):
+        spread(d).wait_send()
+        share_out(d).wait_send()
+    for k in range(docs_here):
+
+        @pl.when(targets[k] != index)
+        def _(k=k):
+            send_query(k).wait_send()
+
+
+def cross_queries(docs_here, context, wo, hidden, gain, wq):
+    size = lax.axis_size("head")
+    rows, features = hidden.shape
+    share = features // size
+    width = wq.shape[1]
+    return pl.pallas_call(
+        functools.partial(cross_query_kernel, docs_here),
+        out_shape=jax.ShapeDtypeStruct((BEAMS, rows, width), jnp.bfloat16),
+        in_specs=[pl.BlockSpec(memory_space=pltpu.VMEM)] * 5,
+        out_specs=pl.BlockSpec(memory_space=pltpu.VMEM),
+        scratch_shapes=[
+            pltpu.VMEM((size, rows, share), jnp.bfloat16),
+            pltpu.VMEM((size - 1, rows, share), jnp.bfloat16),
+            pltpu.VMEM((size, rows, share), jnp.bfloat16),
+            pltpu.VMEM((rows, width), jnp.bfloat16),
+            pltpu.SemaphoreType.DMA((size - 1,)),
+            pltpu.SemaphoreType.DMA((size - 1,)),
+            pltpu.SemaphoreType.DMA((size - 1,)),
+            pltpu.SemaphoreType.DMA((size - 1,)),
+            pltpu.SemaphoreType.DMA((docs_here,)),
+            pltpu.SemaphoreType.DMA((BEAMS,)),
+        ],
+        compiler_params=pltpu.CompilerParams(
+            collective_id=0, has_side_effects=True, vmem_limit_bytes=32 * 1024 * 1024
+        ),
+        cost_estimate=pl.CostEstimate(
+            flops=4 * rows * features * width, bytes_accessed=4 * features * width, transcendentals=0
+        ),
+    )(context, wo, hidden, gain.reshape(1, features), wq)
 
 
 def shards(
@@ -111,7 +274,6 @@
     parents,
 ):
     hyp_count = lax.axis_size("hyp")
-    head_parts = lax.axis_size("head")
     group_size = hyp_count // BEAMS
     my_index = lax.axis_index("hyp")
     my_beam = my_index // group_size
@@ -127,7 +289,6 @@
     beam_groups = [[b * group_size + s for b in range(BEAMS)] for s in range(group_size)]
 
     cross_kv = project_rows(encoder_rows, cross_wkv)
-    cross_kv = cross_kv.reshape(encoder_rows.shape[0], heads, 2, HEAD)
 
     my_langs = lax.dynamic_slice_in_dim(lang_ids, my_slot * docs_here, docs_here, 0).reshape(rows)
     one_hot = (
@@ -218,34 +379,14 @@
         contexts.append((context / total[..., None]).reshape(rows, head_width))
     self_context = jnp.concatenate(contexts, axis=0).astype(jnp.bfloat16)
 
-    partial_out = jnp.dot(self_context, self_wo, preferred_element_type=jnp.float32).astype(
-        jnp.bfloat16
-    )
-    share = features // head_parts
-    spread = lax.all_to_all(
-        partial_out.reshape(STEPS * rows, head_parts, share).transpose(1, 0, 2),
-        "head", 0, 0, tiled=True,
-    )
-    own_sum = jnp.sum(spread.astype(jnp.float32), axis=0).astype(jnp.bfloat16)
-    full_sum = lax.all_gather(own_sum, "head", axis=1, tiled=True)
-    residual = hidden_in + full_sum.astype(jnp.float32)
-    normed_cross = rms_scaled(residual, cross_gain).astype(jnp.bfloat16)
-    cross_query = jnp.dot(normed_cross, cross_wq, preferred_element_type=jnp.float32).astype(
-        jnp.bfloat16
-    )
-
-    by_doc = cross_query.reshape(STEPS, docs_here, targets, head_width).transpose(1, 0, 2, 3)
-    by_doc = by_doc.reshape(1, docs_here, STEPS * targets, head_width)
+    arrived = cross_queries(docs_here, self_context, self_wo, hidden_in, cross_gain, cross_wq)
+    doc_queries = lax.dynamic_index_in_dim(
+        arrived.reshape(BEAMS, STEPS, docs_here, targets, head_width),
+        my_index % docs_here, 2, False,
+    ).reshape(BEAMS * STEPS * targets, head_width)
+    source_slot = my_index // docs_here
     slots = jnp.arange(group_size)
-    outgoing = jnp.where(
-        (slots == my_slot)[:, None, None, None], by_doc, jnp.zeros((), by_doc.dtype)
-    ).reshape(hyp_count, STEPS * targets, head_width)
-    incoming = lax.all_to_all(outgoing, "hyp", 0, 0, tiled=True)
-    source_slot = my_index // docs_here
-    doc_queries = lax.dynamic_index_in_dim(
-        incoming.reshape(BEAMS, group_size, STEPS * targets, head_width), source_slot, 1, False
-    ).reshape(BEAMS * STEPS * targets, head_width)
-    answer = cross_attend(doc_queries, cross_kv[:, :, 0, :], cross_kv[:, :, 1, :], doc_lengths[0])
+    answer = cross_attend(doc_queries, cross_kv, doc_lengths[0])
 
     by_beam = answer.reshape(BEAMS, 1, STEPS * targets, head_width)
     outgoing = jnp.where(

time: 213 us -> 244 us (1.15)
  Pallas kernels: 0 us -> 24.7 us
  other arithmetic: 21.6 us -> 44.9 us
  starting transfers between devices: 33.4 us -> 17.7 us
  matrix products: 37.2 us -> 23.6 us
  local copies, waits for them, and re-layouts: 31.2 us -> 42.4 us
  blocking collectives: 28.9 us -> 33 us
  waiting for transfers between devices: 43.5 us -> 40.5 us
    pallas_call x0 -> x1, Pallas kernels: none -> 24.7 us  [cross_queries(): pl.pallas_call(functools.partial(cross_query_kernel, docs_here), out_shap...]
    all_gather x1, blocking collectives: 13.7 us -> 33 us  [shards(): lax.all_gather(jnp.concatenate(made, axis=1), 'hyp', axis=0, tiled=False,...]
    all_gather x1 -> x0, blocking collectives: 15.2 us -> none  [shards(): full_sum = lax.all_gather(own_sum, 'head', axis=1, tiled=True)]
    dot_general x11 -> x6, matrix products: 30.6 us -> 16.7 us  [the longest x2 15.5 us: project_rows(): jnp.dot(part, full_weights, preferred_element_type=jnp.float32)]
    another operation x2 -> x4, other arithmetic: 1.76 us -> 14.7 us  [the longest x2 12.7 us: gather_weights(): blocks = jnp.stack([low, high], axis=1).reshape((-1,) + block.shape)]
    ppermute x6 -> x3, starting transfers between devices: 13.8 us -> 2.5 us  [gather_weights(): arrived = lax.ppermute(blocks, 'hyp', [(i, i ^ bit) for i in range(size)])]
    ppermute x6 -> x3, waiting for transfers between devices: 25.8 us -> 35.2 us  [gather_weights(): arrived = lax.ppermute(blocks, 'hyp', [(i, i ^ bit) for i in range(size)])]
    unnamed x79 -> x106, local copies, waits for them, and re-layouts: 7.19 us -> 15.9 us
  transfers between devices with their start and end apart: 15 -> 11, of which waited for: 5 -> 2; matrix products, arithmetic and copies ran while one was open for 38% -> 37% of each run, Pallas kernels for 0% -> 10%
where the time goes in v2:
time: 244 us; the launch traced here: 243 us
  other arithmetic  44.9 us (18%)
  local copies, waits for them, and re-layouts  42.4 us (17%)
  waiting for transfers between devices  40.5 us (17%)
  blocking collectives  33 us (14%)
  Pallas kernels  24.7 us (10%)
  matrix products  23.6 us (10%)
  starting transfers between devices  17.7 us (7%)
  between operations  15.8 us (6%)
    ppermute x3, waiting for transfers between devices, gather_weights(): arrived = lax.ppermute(blocks, 'hyp', [(i, i ^ bit) for i in range(size)])  35.2 us
    all_gather x1, blocking collectives, shards(): lax.all_gather(jnp.concatenate(made, axis=1), 'hyp', axis=0, tiled=False,...  33 us
    pallas_call x1, Pallas kernels, cross_queries(): pl.pallas_call(functools.partial(cross_query_kernel, docs_here), out_shap...  24.7 us
    unnamed x106, local copies, waits for them, and re-layouts  15.9 us
    dot_general x2, matrix products, project_rows(): jnp.dot(part, full_weights, preferred_element_type=jnp.float32)  15.5 us
    another operation x2, other arithmetic, gather_weights(): blocks = jnp.stack([low, high], axis=1).reshape((-1,) + block.shape)  12.7 us
    select_n x4, other arithmetic, choose(): jnp.where(flags.reshape(flags.shape + (1,) * (first.ndim - flags.ndim)),...  7.89 us
    ppermute x4, starting transfers between devices, swap(): return lax.ppermute(block, 'hyp', route)  7.6 us
  transfers between devices with their start and end apart: 11, of which 2 were waited for; matrix products, arithmetic and copies ran while one was open for 37% of the time, Pallas kernels for 10%

profile of v2, /device:TPU:0, one launch (start us, length us, event | category | flops | bytes accessed | tf_op | source)
XLA Modules:
  0.0 242.6 jit_solution(8795884444991968562)
XLA Ops:
  7.3 2.8 %fusion.73 = (bf16[384,1024]{1,0:T(8,128)(2,1)}, bf16[384,1024]{1,0:T(8,128)(2,1)}) fusion(bf16[768,1024]{1,0:T(8,128)(2,1)} %param.27), kind=kLoop, calls=%fused_computation.218 | loop fusion | bytes 3145728 | tf_op jit(solution)/shard_map/slice | solution.py:97
  11.2 3.0 %collective-permute-start.5 = (bf16[16,32,512]{2,0,1:T(8,128)(2,1)}, bf16[16,32,512]{2,0,1:T(8,128)(2,1)}, u32[]{:S(2)}, u32[]{:S(2)}) collective-permute-start(bf16[16,32,512]{2,0,1:T(8,128)(2,1)} %copy.176), channel_id=1, source_target_pairs={{0,16},{4,20},{8,24},{12,28},{16,0},{20,4},{24,8},{28,12},{1,17},{... | collective-permute-start | bytes 1572872 | tf_op jit(solution)/shard_map/ppermute | solution.py:40
  18.2 3.5 %convolution_convert_fusion.2 = bf16[48,512]{1,0:T(8,128)(2,1)S(1)} fusion(bf16[48,4096]{1,0:T(8,128)(2,1)S(1)} %multiply_convert_fusion, bf16[4096,512]{1,0:T(8,128)(2,1)} %param.22), kind=kOutput, calls=%fused_computation.23 | convolution fusion | flops 201351168 | bytes 4636672 | tf_op jit(solution)/shard_map/dot_general | solution.py:301
  24.5 33.0 %all-gather = bf16[192,1536]{1,0:T(8,128)(2,1)S(1)} all-gather(bf16[48,1536]{1,0:T(8,128)(2,1)S(1)} %pad_maximum_fusion.8), channel_id=2, replica_groups={{0,8,16,24},{4,12,20,28},{1,9,17,25},{5,13,21,29},{2,10,18,26},{6,14,22..., dimensions={0}, use_global_device_ids=true | all-gather | bytes 737280 | tf_op jit(solution)/shard_map/all_gather | solution.py:304
  57.9 2.0 fusion.74
  64.4 4.2 %all-to-all-start = ((f32[4,48,516]{2,1,0:T(8,128)}), f32[4,48,516]{2,1,0:T(8,128)}, u32[]{:S(2)}, u32[]{:S(2)}) async-start(f32[4,48,516]{2,1,0:T(8,128)} %pad_maximum_fusion.5), calls=%async_computation | async-start | bytes 983040 | tf_op jit(solution)/shard_map/all_to_all | solution.py:343
  69.6 1.7 broadcast_select_fusion.3
  73.8 2.0 collective-permute-start.1
  84.8 35.2 %collective-permute-done.1 = bf16[2,512,1024]{2,1,0:T(8,128)(2,1)} collective-permute-done((bf16[2,512,1024]{2,1,0:T(8,128)(2,1)}, bf16[2,512,1024]{2,1,0:T(8,128)(2,1)}, u32[]{:S(2)}, u32[]{:S(2)}) %collective-permute-start.1) | collective-permute-done | bytes 2097184 | tf_op jit(solution)/shard_map/ppermute | solution.py:82
  120.0 2.5 %broadcast_select_fusion.1 = (bf16[2,512,1024]{2,1,0:T(8,128)(2,1)S(1)}, bf16[2,512,1024]{2,1,0:T(8,128)(2,1)S(1)}) fusion(bf16[2,512,1024]{2,1,0:T(8,128)(2,1)} %collective-permute-done.1, pred[]{:T(512)S(6)} %ne.77, bf16[1,512,1024]{2,1,0:T(8,128)(2,1)} %copy-done.8, bf16[1,512,1024]{2,1,0:T(8,128)(2,1)} %copy-done.7), kind=kLoop, calls=%fused_computation.6 | loop fusion | flops 3145728 | bytes 8388609 | tf_op jit(solution)/shard_map/jit(_where)/select_n | solution.py:84
  122.5 2.4 pad_maximum_fusion.1
  154.1 2.2 broadcast_select_fusion.4
  156.2 1.7 collective-permute-start.6
  157.9 2.3 broadcast_select_fusion.5
  161.7 2.2 copy-done.2
  163.9 2.2 copy-done.3
  166.1 24.7 %shard_map.175 = bf16[4,48,512]{2,1,0:T(8,128)(2,1)S(1)} custom-call(bf16[48,512]{1,0:T(8,128)(2,1)S(1)} %pad_maximum_fusion.10.context, bf16[512,4096]{1,0:T(8,128)(2,1)S(1)} %copy-done.2, f32[48,4096]{1,0:T(8,128)S(1)} %bitcast.323, f32[1,4096]{1,0:T(1,128)S(1)} %bitcast.324, bf16[4096,512]{1,0:T(8,128)(2,1)S(1)} %copy-done.3), custom_call_target="tpu_custom_call" | custom-call | flops 402653184 | bytes 8388608 | tf_op jit(solution)/shard_map/pallas_call | solution.py:232
  191.0 1.9 select_select_fusion
  195.4 5.2 %select_bitcast_fusion.1 = (bf16[4,1,512,1024]{3,2,1,0:T(8,128)(2,1)}, bf16[4,1,512,1024]{3,2,1,0:T(8,128)(2,1)}) fusion(bf16[4,512,1024]{2,1,0:T(8,128)(2,1)} %collective-permute-done.2, pred[]{:T(512)S(6)} %ne.76, bf16[2,512,1024]{2,1,0:T(8,128)(2,1)S(1)} %copy-done.6, bf16[2,512,1024]{2,1,0:T(8,128)(2,1)S(1)} %get-tuple-element.28), kind=kLoop, calls=%fused_computation.3 | loop fusion | flops 6291456 | bytes 16777216 | tf_op jit(solution)/shard_map/stack | solution.py:89
  200.5 7.5 %pad_maximum_fusion = bf16[4,2,512,1024]{3,2,1,0:T(8,128)(2,1)} fusion(bf16[4,1,512,1024]{3,2,1,0:T(8,128)(2,1)} %get-tuple-element.27, bf16[4,1,512,1024]{3,2,1,0:T(8,128)(2,1)} %get-tuple-element.26), kind=kLoop, calls=%fused_computation | loop fusion | flops 4194304 | bytes 16777216 | tf_op jit(solution)/shard_map/stack | solution.py:89
  208.1 7.7 %fusion = bf16[384,1024]{1,0:T(8,128)(2,1)S(1)} fusion(bf16[384,4096]{1,0:T(8,128)(2,1)} %all-gather.4.cloned.1.call-done, bf16[4096,1024]{1,0:T(8,128)(2,1)} %bitcast.325), kind=kOutput, calls=%fused_computation.15 | convolution fusion | flops 3221618688 | bytes 12320768 | tf_op jit(solution)/shard_map/dot_general | solution.py:103
  215.9 7.7 %fusion.1 = bf16[384,1024]{1,0:T(8,128)(2,1)S(1)} fusion(bf16[384,4096]{1,0:T(8,128)(2,1)} %all-gather.6.cloned.1.call-done, bf16[4096,1024]{1,0:T(8,128)(2,1)} %bitcast.326), kind=kOutput, calls=%fused_computation.16 | convolution fusion | flops 3221618688 | bytes 12320768 | tf_op jit(solution)/shard_map/dot_general | solution.py:103
  226.2 3.4 %all-to-all-start.1 = ((bf16[8,12,512]{2,1,0:T(8,128)(2,1)}), bf16[8,12,512]{2,1,0:T(8,128)(2,1)S(1)}, u32[]{:S(2)}, u32[]{:S(2)}) async-start(bf16[8,12,512]{2,1,0:T(8,128)(2,1)} %bitcast_select_fusion), calls=%async_computation.1 | async-start | bytes 262144 | tf_op jit(solution)/shard_map/all_to_all | solution.py:395
  230.5 4.5 %all-to-all-done.1 = bf16[8,12,512]{2,1,0:T(8,128)(2,1)S(1)} async-done(((bf16[8,12,512]{2,1,0:T(8,128)(2,1)}), bf16[8,12,512]{2,1,0:T(8,128)(2,1)S(1)}, u32[]{:S(2)}, u32[]{:S(2)}) %all-to-all-start.1) | async-done | bytes 98336 | tf_op jit(solution)/shard_map/all_to_all | solution.py:395
  (249 shorter events, 61.5 us)
Async XLA Ops:
  7.2 200.9 %all-gather.4.cloned.1.call-start = ((), (), s32[]{:S(2)}) async-start(), calls=%async_computation.2 | async-start | bytes 3932160 | tf_op jit(solution)/shard_map/all_gather | solution.py:97
  11.2 142.9 %collective-permute-start.5 = (bf16[16,32,512]{2,0,1:T(8,128)(2,1)}, bf16[16,32,512]{2,0,1:T(8,128)(2,1)}, u32[]{:S(2)}, u32[]{:S(2)}) collective-permute-start(bf16[16,32,512]{2,0,1:T(8,128)(2,1)} %copy.176), channel_id=1, source_target_pairs={{0,16},{4,20},{8,24},{12,28},{16,0},{20,4},{24,8},{28,12},{1,17},{... | collective-permute-start | bytes 1572872 | tf_op jit(solution)/shard_map/ppermute | solution.py:40
  15.2 142.7 %collective-permute-start.3 = (bf16[16,32,512]{2,0,1:T(8,128)(2,1)}, bf16[16,32,512]{2,0,1:T(8,128)(2,1)}, u32[]{:S(2)}, u32[]{:S(2)}) collective-permute-start(bf16[16,32,512]{2,0,1:T(8,128)(2,1)} %copy.173), channel_id=1, source_target_pairs={{0,8},{4,12},{8,0},{12,4},{16,24},{20,28},{24,16},{28,20},{1,9},{5... | collective-permute-start | bytes 1572872 | tf_op jit(solution)/shard_map/ppermute | solution.py:40
  16.7 52.9 %collective-permute-start = (bf16[1,512,1024]{2,1,0:T(8,128)(2,1)}, bf16[1,512,1024]{2,1,0:T(8,128)(2,1)}, u32[]{:S(2)}, u32[]{:S(2)}) collective-permute-start(bf16[1,512,1024]{2,1,0:T(8,128)(2,1)} %bitcast.329), channel_id=1, source_target_pairs={{0,8},{4,12},{8,0},{12,4},{16,24},{20,28},{24,16},{28,20},{1,9},{5... | collective-permute-start | bytes 3145736 | tf_op jit(solution)/shard_map/ppermute | solution.py:82
  64.4 63.9 %all-to-all-start = ((f32[4,48,516]{2,1,0:T(8,128)}), f32[4,48,516]{2,1,0:T(8,128)}, u32[]{:S(2)}, u32[]{:S(2)}) async-start(f32[4,48,516]{2,1,0:T(8,128)} %pad_maximum_fusion.5), calls=%async_computation | async-start | bytes 983040 | tf_op jit(solution)/shard_map/all_to_all | solution.py:343
  68.6 147.3 %all-gather.6.cloned.1.call-start = ((), (), s32[]{:S(2)}) async-start(), calls=%async_computation.3 | async-start | bytes 3932160 | tf_op jit(solution)/shard_map/all_gather | solution.py:97
  73.8 46.1 %collective-permute-start.1 = (bf16[2,512,1024]{2,1,0:T(8,128)(2,1)}, bf16[2,512,1024]{2,1,0:T(8,128)(2,1)}, u32[]{:S(2)}, u32[]{:S(2)}) collective-permute-start(bf16[2,512,1024]{2,1,0:T(8,128)(2,1)} %pad_maximum_fusion.2), channel_id=1, source_target_pairs={{0,16},{4,20},{8,24},{12,28},{16,0},{20,4},{24,8},{28,12},{1,17},{... | collective-permute-start | bytes 6291464 | tf_op jit(solution)/shard_map/ppermute | solution.py:82
  76.9 50.7 %copy-start.28 = (pred[16]{0:T(512)(128)(4,1)}, pred[16]{0:T(512)(128)(4,1)S(1)}, u32[]{:S(2)}) copy-start(pred[16]{0:T(512)(128)(4,1)S(1)} %get-tuple-element.92) | copy-start | bytes 52
  76.9 50.7 %copy-start.29 = (pred[16]{0:T(512)(128)(4,1)}, pred[16]{0:T(512)(128)(4,1)S(1)}, u32[]{:S(2)}) copy-start(pred[16]{0:T(512)(128)(4,1)S(1)} %get-tuple-element.93) | copy-start | bytes 52
  76.9 50.7 %copy-start.30 = (pred[16]{0:T(512)(128)(4,1)}, pred[16]{0:T(512)(128)(4,1)S(1)}, u32[]{:S(2)}) copy-start(pred[16]{0:T(512)(128)(4,1)S(1)} %get-tuple-element.94) | copy-start | bytes 52
  77.0 50.6 %copy-start.31 = (pred[16]{0:T(512)(128)(4,1)}, pred[16]{0:T(512)(128)(4,1)S(1)}, u32[]{:S(2)}) copy-start(pred[16]{0:T(512)(128)(4,1)S(1)} %get-tuple-element.89) | copy-start | bytes 52
  77.0 50.6 %copy-start.32 = (pred[16]{0:T(512)(128)(4,1)}, pred[16]{0:T(512)(128)(4,1)S(1)}, u32[]{:S(2)}) copy-start(pred[16]{0:T(512)(128)(4,1)S(1)} %get-tuple-element.90) | copy-start | bytes 52
  77.0 50.6 %copy-start.33 = (pred[16]{0:T(512)(128)(4,1)}, pred[16]{0:T(512)(128)(4,1)S(1)}, u32[]{:S(2)}) copy-start(pred[16]{0:T(512)(128)(4,1)S(1)} %get-tuple-element.91) | copy-start | bytes 52
  125.1 36.5 %copy-start.4 = (f32[4096]{0:T(1024)S(1)}, f32[4096]{0:T(1024)}, u32[]{:S(2)}) copy-start(f32[4096]{0:T(1024)} %param.24) | copy-start | bytes 49156
  125.2 70.2 %collective-permute-start.2 = (bf16[4,512,1024]{2,1,0:T(8,128)(2,1)}, bf16[4,512,1024]{2,1,0:T(8,128)(2,1)}, u32[]{:S(2)}, u32[]{:S(2)}) collective-permute-start(bf16[4,512,1024]{2,1,0:T(8,128)(2,1)} %pad_maximum_fusion.1), channel_id=1, source_target_pairs={{0,4},{4,0},{8,12},{12,8},{16,20},{20,16},{24,28},{28,24},{1,5},{5... | collective-permute-start | bytes 12582920 | tf_op jit(solution)/shard_map/ppermute | solution.py:82
  156.2 34.7 %collective-permute-start.6 = (bf16[16,32,512]{2,0,1:T(8,128)(2,1)}, bf16[16,32,512]{2,0,1:T(8,128)(2,1)}, u32[]{:S(2)}, u32[]{:S(2)}) collective-permute-start(bf16[16,32,512]{2,0,1:T(8,128)(2,1)} %broadcast_select_fusion.4), channel_id=1, source_target_pairs={{0,8},{4,12},{8,0},{12,4},{16,24},{20,28},{24,16},{28,20},{1,9},{5... | collective-permute-start | bytes 1572872 | tf_op jit(solution)/shard_map/ppermute | solution.py:40
  160.2 33.6 %collective-permute-start.4 = (bf16[16,32,512]{2,0,1:T(8,128)(2,1)}, bf16[16,32,512]{2,0,1:T(8,128)(2,1)}, u32[]{:S(2)}, u32[]{:S(2)}) collective-permute-start(bf16[16,32,512]{2,0,1:T(8,128)(2,1)} %broadcast_select_fusion.5), channel_id=1, source_target_pairs={{0,16},{4,20},{8,24},{12,28},{16,0},{20,4},{24,8},{28,12},{1,17},{... | collective-permute-start | bytes 1572872 | tf_op jit(solution)/shard_map/ppermute | solution.py:40
  166.1 24.9 %copy-start.41 = (pred[16]{0:T(512)(128)(4,1)S(1)}, pred[16]{0:T(512)(128)(4,1)}, u32[]{:S(2)}) copy-start(pred[16]{0:T(512)(128)(4,1)} %get-tuple-element.87) | copy-start | bytes 52
  166.1 26.8 %copy-start.21 = (bf16[16,1,512]{2,0,1:T(8,128)(2,1)S(1)}, bf16[16,1,512]{2,0,1:T(8,128)(2,1)}, u32[]{:S(2)}) copy-start(bf16[16,1,512]{2,0,1:T(8,128)(2,1)} %dynamic-slice_bitcast_fusion) | copy-start | bytes 49156
  166.1 26.8 %copy-start.25 = (bf16[16,1,512]{2,0,1:T(8,128)(2,1)S(1)}, bf16[16,1,512]{2,0,1:T(8,128)(2,1)}, u32[]{:S(2)}) copy-start(bf16[16,1,512]{2,0,1:T(8,128)(2,1)} %get-tuple-element.43) | copy-start | bytes 49156
  166.1 26.8 %copy-start.26 = (bf16[16,1,512]{2,0,1:T(8,128)(2,1)S(1)}, bf16[16,1,512]{2,0,1:T(8,128)(2,1)}, u32[]{:S(2)}) copy-start(bf16[16,1,512]{2,0,1:T(8,128)(2,1)} %get-tuple-element.44) | copy-start | bytes 49156
  166.1 27.7 %copy-start.38 = (pred[16]{0:T(512)(128)(4,1)S(1)}, pred[16]{0:T(512)(128)(4,1)}, u32[]{:S(2)}) copy-start(pred[16]{0:T(512)(128)(4,1)} %get-tuple-element.102) | copy-start | bytes 52
  166.1 27.7 %copy-start.39 = (pred[16]{0:T(512)(128)(4,1)S(1)}, pred[16]{0:T(512)(128)(4,1)}, u32[]{:S(2)}) copy-start(pred[16]{0:T(512)(128)(4,1)} %get-tuple-element.103) | copy-start | bytes 52
  226.2 8.8 %all-to-all-start.1 = ((bf16[8,12,512]{2,1,0:T(8,128)(2,1)}), bf16[8,12,512]{2,1,0:T(8,128)(2,1)S(1)}, u32[]{:S(2)}, u32[]{:S(2)}) async-start(bf16[8,12,512]{2,1,0:T(8,128)(2,1)} %bitcast_select_fusion), calls=%async_computation.1 | async-start | bytes 262144 | tf_op jit(solution)/shard_map/all_to_all | solution.py:395
  (32 other events, 213.7 us)
Sparse Core Ops, SparseCore 0:
  10.2 66.1 all-gather.3
  78.0 62.1 all-gather.5

commit v3 on v2

--- a/solution.py
+++ b/solution.py
@@ -53,58 +53,94 @@
     return choose((my_rows & other) == (my_beam & other), local, arrived)
 
 
-def cross_attend(queries, cross_kv, doc_length):
-    rows = cross_kv.shape[0]
-    live_mask = lax.broadcasted_iota(jnp.int32, (1, rows), 1) < doc_length
-    outputs = []
-    for head in range(queries.shape[1] // HEAD):
-        query = queries[:, head * HEAD : (head + 1) * HEAD]
-        keys = cross_kv[:, 2 * head * HEAD : (2 * head + 1) * HEAD]
-        values = cross_kv[:, (2 * head + 1) * HEAD : (2 * head + 2) * HEAD]
+def document_kernel(size, *refs):
+    pieces, (weights, queries, length, out) = refs[: 2 * size - 1], refs[2 * size - 1 : 2 * size + 3]
+    rows_all, weights_all, cross_kv, piece_sem, weight_sem = refs[2 * size + 3 :]
+    me = lax.axis_index("head")
+    width = pieces[0].shape[1]
+    tiles = cross_kv.shape[0]
+
+    def copy(position, owner):
+        columns = pl.ds(pl.multiple_of(owner * width, width), width)
+        return pltpu.make_async_copy(
+            pieces[position], rows_all.at[:, columns], piece_sem.at[position]
+        )
+
+    def each(action):
+        action(copy(0, me))
+        for step in range(1, size):
+
+            @pl.when(me >= step)
+            def _():
+                action(copy(step, me - step))
+
+            @pl.when(me + step < size)
+            def _():
+                action(copy(size - 1 + step, me + step))
+
+    whole = pltpu.make_async_copy(weights, weights_all, weight_sem)
+    whole.start()
+    each(lambda item: item.start())
+    whole.wait()
+    each(lambda item: item.wait())
+
+    def project(tile, carry):
+        columns = pl.ds(pl.multiple_of(tile * HEAD, HEAD), HEAD)
+        cross_kv[tile] = jnp.dot(
+            rows_all[...], weights_all[:, columns], preferred_element_type=jnp.float32
+        ).astype(jnp.bfloat16)
+        return carry
+
+    lax.fori_loop(0, tiles, project, 0)
+    live = lax.broadcasted_iota(jnp.int32, (1, cross_kv.shape[1]), 1) < length[0]
+    for head in range(tiles // 2):
+        columns = slice(head * HEAD, (head + 1) * HEAD)
         scores = lax.dot_general(
-            query, keys, (((1,), (1,)), ((), ())), preferred_element_type=jnp.float32
+            queries[:, columns], cross_kv[2 * head], (((1,), (1,)), ((), ())),
+            preferred_element_type=jnp.float32,
         ) * (HEAD ** (-0.5))
-        scores = jnp.where(live_mask, scores, -jnp.inf)
+        scores = jnp.where(live, scores, -jnp.inf)
         raw_weights = jnp.exp(scores - jnp.max(scores, axis=1, keepdims=True))
         totals = jnp.sum(raw_weights, axis=1, keepdims=True)
-        weights = (raw_weights / totals).astype(jnp.bfloat16)
-        outputs.append(jnp.dot(weights, values, preferred_element_type=jnp.float32))
-    return jnp.concatenate(outputs, axis=1).astype(jnp.bfloat16)
-
-
-def gather_weights(block):
-    size = lax.axis_size("hyp")
-    me = lax.axis_index("hyp")
-    blocks = block[None]
-    bits = [1 << k for k in range(1, size.bit_length() - 1)] + [1]
-    done = 0
-    for bit in bits:
-        arrived = lax.ppermute(blocks, "hyp", [(i, i ^ bit) for i in range(size)])
-        mine_high = (me & bit) != 0
-        low = jnp.where(mine_high, arrived, blocks)
-        high = jnp.where(mine_high, blocks, arrived)
-        if bit > done:
-            blocks = jnp.concatenate([low, high], axis=0)
-        else:
-            blocks = jnp.stack([low, high], axis=1).reshape((-1,) + block.shape)
-        done = max(done, bit)
-    return blocks.reshape(size * block.shape[0], block.shape[1])
-
-
-def project_rows(encoder_rows, cross_wkv):
-    half = encoder_rows.shape[0] // 2
-    parts = [
-        lax.all_gather(encoder_rows[k * half : (k + 1) * half], "head", axis=1, tiled=True)
-        for k in range(2)
-    ]
-    full_weights = gather_weights(cross_wkv)
-    return jnp.concatenate(
-        [
-            jnp.dot(part, full_weights, preferred_element_type=jnp.float32).astype(jnp.bfloat16)
-            for part in parts
+        probs = (raw_weights / totals).astype(jnp.bfloat16)
+        out[:, columns] = jnp.dot(
+            probs, cross_kv[2 * head + 1], preferred_element_type=jnp.float32
+        ).astype(jnp.bfloat16)
+
+
+def document_attend(pieces, weights, queries, length):
+    size = lax.axis_size("head")
+    rows = pieces[0].shape[0]
+    features, columns = weights.shape
+    anywhere = pl.BlockSpec(memory_space=pl.ANY)
+    return pl.pallas_call(
+        functools.partial(document_kernel, size),
+        out_shape=jax.ShapeDtypeStruct(queries.shape, jnp.bfloat16),
+        in_specs=[anywhere] * (len(pieces) + 1)
+        + [pl.BlockSpec(memory_space=pltpu.VMEM), pl.BlockSpec(memory_space=pltpu.SMEM)],
+        out_specs=pl.BlockSpec(memory_space=pltpu.VMEM),
+        scratch_shapes=[
+            pltpu.VMEM((rows, features), jnp.bfloat16),
+            pltpu.VMEM((features, columns), jnp.bfloat16),
+            pltpu.VMEM((columns // HEAD, rows, HEAD), jnp.bfloat16),
+            pltpu.SemaphoreType.DMA((len(pieces),)),
+            pltpu.SemaphoreType.DMA,
         ],
-        axis=0,
-    )
+        compiler_params=pltpu.CompilerParams(vmem_limit_bytes=40 * 1024 * 1024),
+        cost_estimate=pl.CostEstimate(
+            flops=2 * rows * features * columns,
+            bytes_accessed=2 * features * (rows + columns),
+            transcendentals=0,
+        ),
+    )(*pieces, weights, queries, length)
+
+
+def travel(pair, step):
+    size = lax.axis_size("head")
+    up, down = pair
+    upward = [(i, i + 1) for i in range(step - 1, size - 1)]
+    downward = [(i + 1, i) for i in range(size - step)]
+    return lax.ppermute(up, "head", upward), lax.ppermute(down, "head", downward)
 
 
 def cross_query_kernel(
@@ -250,7 +286,9 @@
             collective_id=0, has_side_effects=True, vmem_limit_bytes=32 * 1024 * 1024
         ),
         cost_estimate=pl.CostEstimate(
-            flops=4 * rows * features * width, bytes_accessed=4 * features * width, transcendentals=0
+            flops=4 * rows * features * width,
+            bytes_accessed=16 * features * width,
+            transcendentals=0,
         ),
     )(context, wo, hidden, gain.reshape(1, features), wq)
 
@@ -288,7 +326,9 @@
     scaling = HEAD ** (-0.5)
     beam_groups = [[b * group_size + s for b in range(BEAMS)] for s in range(group_size)]
 
-    cross_kv = project_rows(encoder_rows, cross_wkv)
+    head_parts = lax.axis_size("head")
+    full_weights = lax.all_gather(cross_wkv, "hyp", axis=0, tiled=True)
+    hops = [travel((encoder_rows, encoder_rows), 1)]
 
     my_langs = lax.dynamic_slice_in_dim(lang_ids, my_slot * docs_here, docs_here, 0).reshape(rows)
     one_hot = (
@@ -303,7 +343,13 @@
     ]
     every = lax.all_gather(
         jnp.concatenate(made, axis=1), "hyp", axis=0, tiled=False, axis_index_groups=beam_groups
-    ).reshape(BEAMS, STEPS, rows, 3, head_width)
+    )
+    every, hops[0], late_keys, late_values = lax.optimization_barrier(
+        (every, hops[0], past_keys, past_values)
+    )
+    every = every.reshape(BEAMS, STEPS, rows, 3, head_width)
+    for step in range(2, max(head_parts - 1, 2)):
+        hops.append(travel(hops[-1], step))
     queries, keys, values = every[:, :, :, 0], every[:, :, :, 1], every[:, :, :, 2]
 
     parent_view = parents.reshape(STEPS, BEAMS, -1)
@@ -379,6 +425,9 @@
         contexts.append((context / total[..., None]).reshape(rows, head_width))
     self_context = jnp.concatenate(contexts, axis=0).astype(jnp.bfloat16)
 
+    self_context, hops[-1] = lax.optimization_barrier((self_context, hops[-1]))
+    for step in range(len(hops) + 1, head_parts):
+        hops.append(travel(hops[-1], step))
     arrived = cross_queries(docs_here, self_context, self_wo, hidden_in, cross_gain, cross_wq)
     doc_queries = lax.dynamic_index_in_dim(
         arrived.reshape(BEAMS, STEPS, docs_here, targets, head_width),
@@ -386,7 +435,8 @@
     ).reshape(BEAMS * STEPS * targets, head_width)
     source_slot = my_index // docs_here
     slots = jnp.arange(group_size)
-    answer = cross_attend(doc_queries, cross_kv, doc_lengths[0])
+    pieces = [encoder_rows] + [up for up, _ in hops] + [down for _, down in hops]
+    answer = document_attend(pieces[: 2 * head_parts - 1], full_weights, doc_queries, doc_lengths)
 
     by_beam = answer.reshape(BEAMS, 1, STEPS * targets, head_width)
     outgoing = jnp.where(
@@ -401,8 +451,8 @@
     )
 
     last = ancestors[STEPS - 1][-1]
-    out_keys = final_cache(past_keys, 1, my_beam, last, group_size)
-    out_values = final_cache(past_values, 2, my_beam, last, group_size)
+    out_keys = final_cache(late_keys, 1, my_beam, last, group_size)
+    out_values = final_cache(late_values, 2, my_beam, last, group_size)
     final_keys = jnp.concatenate([out_keys, jnp.stack(last_keys, axis=1)], axis=1)
     final_values = jnp.concatenate([out_values, jnp.stack(last_values, axis=1)], axis=1)
     return (cross_context, final_keys, final_values)

time: 244 us -> 248 us (1.016)
  local copies, waits for them, and re-layouts: 42.4 us -> 76.5 us
  Pallas kernels: 24.7 us -> 51.3 us
  blocking collectives: 33 us -> 14.1 us
  waiting for transfers between devices: 40.5 us -> 22.1 us
  matrix products: 23.6 us -> 8.48 us
  other arithmetic: 44.9 us -> 32.7 us
  starting transfers between devices: 17.7 us -> 24.6 us
    ppermute x3 -> x6, waiting for transfers between devices: 35.2 us -> 8.06 us  [the longest x3 4.22 us: travel(): lax.ppermute(down, 'head', downward)]
    all_gather x1, blocking collectives: 33 us -> 14.1 us  [shards(): lax.all_gather(jnp.concatenate(made, axis=1), 'hyp', axis=0, tiled=False,...]
    dot_general x6 -> x0, matrix products: 16.7 us -> none  [the longest x2 15.5 us: project_rows(): jnp.dot(part, full_weights, preferred_element_type=jnp.float32)]
    pallas_call x0 -> x1, Pallas kernels: none -> 13.4 us  [document_attend(): pl.pallas_call(functools.partial(document_kernel, size), out_shape=jax.Sh...]
    pallas_call x1, Pallas kernels: 24.7 us -> 38 us  [cross_queries(): pl.pallas_call(functools.partial(cross_query_kernel, docs_here), out_shap...]
    another operation x4 -> x2, other arithmetic: 14.7 us -> 1.89 us  [the longest x2 12.7 us: gather_weights(): blocks = jnp.stack([low, high], axis=1).reshape((-1,) + block.shape)]
    unnamed x106 -> x73, local copies, waits for them, and re-layouts: 15.9 us -> 5.01 us
    ppermute x3 -> x6, starting transfers between devices: 2.5 us -> 12.6 us  [the longest x3 8.74 us: travel(): lax.ppermute(up, 'head', upward)]
  transfers between devices with their start and end apart: 11 -> 13, of which waited for: 2 -> 5; matrix products, arithmetic and copies ran while one was open for 37% -> 46% of each run, Pallas kernels for 10% -> 15%
where the time goes in v3:
time: 248 us; the launch traced here: 245 us
  local copies, waits for them, and re-layouts  76.5 us (31%)
  Pallas kernels  51.3 us (21%)
  other arithmetic  32.7 us (13%)
  starting transfers between devices  24.6 us (10%)
  waiting for transfers between devices  22.1 us (9%)
  between operations  15.5 us (6%)
  blocking collectives  14.1 us (6%)
  matrix products  8.48 us (3%)
    pallas_call x1, Pallas kernels, cross_queries(): pl.pallas_call(functools.partial(cross_query_kernel, docs_here), out_shap...  38 us
    all_gather x1, blocking collectives, shards(): lax.all_gather(jnp.concatenate(made, axis=1), 'hyp', axis=0, tiled=False,...  14.1 us
    pallas_call x1, Pallas kernels, document_attend(): pl.pallas_call(functools.partial(document_kernel, size), out_shape=jax.Sh...  13.4 us
    ppermute x4, waiting for transfers between devices, swap(): return lax.ppermute(block, 'hyp', route)  8.8 us
    ppermute x3, starting transfers between devices, travel(): lax.ppermute(up, 'head', upward)  8.74 us
    exp x6, local copies, waits for them, and re-layouts, shards(): weight = jnp.exp(score - top)  7.82 us
    squeeze x8, local copies, waits for them, and re-layouts, shards(): key = pick([keys[b, j] for b in range(BEAMS)], owner)  7.03 us
    select_n x4, other arithmetic, choose(): jnp.where(flags.reshape(flags.shape + (1,) * (first.ndim - flags.ndim)),...  6.91 us
  transfers between devices with their start and end apart: 13, of which 5 were waited for; matrix products, arithmetic and copies ran while one was open for 46% of the time, Pallas kernels for 15%

profile of v3, /device:TPU:0, one launch (start us, length us, event | category | flops | bytes accessed | tf_op | source)
XLA Modules:
  0.0 245.3 jit_solution(2656890382664637812)
XLA Ops:
  7.9 5.0 %collective-permute-start = (bf16[768,1024]{1,0:T(8,128)(2,1)}, bf16[768,1024]{1,0:T(8,128)(2,1)S(1)}, u32[]{:S(2)}, u32[]{:S(2)}) collective-permute-start(bf16[768,1024]{1,0:T(8,128)(2,1)} %refs_0_.1), channel_id=1, source_target_pairs={{0,1},{1,2},{2,3},{4,5},{5,6},{6,7},{8,9},{9,10},{10,11},{12,13},{... | collective-permute-start | bytes 4718600 | tf_op jit(solution)/shard_map/ppermute | solution.py:143
  19.9 4.1 %convolution_convert_fusion = bf16[48,512]{1,0:T(8,128)(2,1)S(1)} fusion(bf16[48,4096]{1,0:T(8,128)(2,1)S(1)} %multiply_convert_fusion, bf16[4096,512]{1,0:T(8,128)(2,1)} %param.22), kind=kOutput, calls=%fused_computation.2 | convolution fusion | flops 201351168 | bytes 4636672 | tf_op jit(solution)/shard_map/dot_general | solution.py:341
  25.7 14.1 %all-gather = bf16[192,1536]{1,0:T(8,128)(2,1)} all-gather(bf16[48,1536]{1,0:T(8,128)(2,1)S(1)} %pad_maximum_fusion.3), channel_id=2, replica_groups={{0,8,16,24},{4,12,20,28},{1,9,17,25},{5,13,21,29},{2,10,18,26},{6,14,22..., dimensions={0}, use_global_device_ids=true | all-gather | bytes 737280 | tf_op jit(solution)/shard_map/all_gather | solution.py:344
  43.0 3.8 %collective-permute-done.refs_1_ = bf16[768,1024]{1,0:T(8,128)(2,1)S(1)} collective-permute-done((bf16[768,1024]{1,0:T(8,128)(2,1)}, bf16[768,1024]{1,0:T(8,128)(2,1)S(1)}, u32[]{:S(2)}, u32[]{:S(2)}) %collective-permute-start) | collective-permute-done | bytes 1572896 | tf_op jit(solution)/shard_map/ppermute | solution.py:143
  46.8 4.2 %collective-permute-done.1.refs_4_ = bf16[768,1024]{1,0:T(8,128)(2,1)} collective-permute-done((bf16[768,1024]{1,0:T(8,128)(2,1)}, bf16[768,1024]{1,0:T(8,128)(2,1)}, u32[]{:S(2)}, u32[]{:S(2)}) %collective-permute-start.1) | collective-permute-done | bytes 1572896 | tf_op jit(solution)/shard_map/ppermute | solution.py:143
  51.0 2.2 reshape.1085
  53.2 3.2 %fusion.50 = (bf16[4,3,16,1,512]{4,3,2,1,0:T(2,128)(2,1)S(1)}, bf16[4,3,16,1,512]{4,3,2,1,0:T(2,128)(2,1)S(1)}, bf16[4,3,16,1,512]{4,3,2,1,0:T(2,128)(2,1)S(1)}) fusion(bf16[4,3,16,3,512]{4,3,2,1,0:T(4,128)(2,1)} %reshape.1085), kind=kLoop, calls=%fused_computation.170 | loop fusion | bytes 1179648 | tf_op jit(solution)/shard_map/slice | solution.py:353
  66.9 1.6 fusion.54
  70.4 1.7 reshape_squeeze.3
  89.6 2.1 reshape.1088
  91.7 1.9 pad_maximum_fusion.2
  93.5 4.1 %all-to-all-start = ((f32[4,48,516]{2,1,0:T(8,128)}), f32[4,48,516]{2,1,0:T(8,128)}, u32[]{:S(2)}, u32[]{:S(2)}) async-start(f32[4,48,516]{2,1,0:T(8,128)} %pad_maximum_fusion.2), calls=%async_computation | async-start | bytes 983040 | tf_op jit(solution)/shard_map/all_to_all | solution.py:389
  97.7 1.8 multiply_reduce_fusion.5
  108.8 2.0 collective-permute-start.8
  112.2 1.9 collective-permute-start.2
  115.4 1.6 fusion.52
  154.2 1.8 collective-permute-start.4
  159.5 1.8 broadcast_select_fusion.1
  161.9 8.7 %collective-permute-done.9 = bf16[16,32,512]{2,0,1:T(8,128)(2,1)S(1)} collective-permute-done((bf16[16,32,512]{2,0,1:T(8,128)(2,1)S(1)}, bf16[16,32,512]{2,0,1:T(8,128)(2,1)S(1)}, u32[]{:S(2)}, u32[]{:S(2)}) %collective-permute-start.9) | collective-permute-done | bytes 524320 | tf_op jit(solution)/shard_map/ppermute | solution.py:40
  173.0 2.2 select_select_fusion.1
  175.2 38.0 %shard_map.175 = bf16[4,48,512]{2,1,0:T(8,128)(2,1)S(1)} custom-call(bf16[48,512]{1,0:T(8,128)(2,1)S(1)} %pad_maximum_fusion.4.context, bf16[512,4096]{1,0:T(8,128)(2,1)S(1)} %copy-done.1, f32[48,4096]{1,0:T(8,128)S(1)} %bitcast.308, f32[1,4096]{1,0:T(1,128)S(1)} %bitcast.309, bf16[4096,512]{1,0:T(8,128)(2,1)S(1)} %copy-done.2), custom_call_target="tpu_custom_call" | custom-call | flops 402653184 | bytes 33554432 | tf_op jit(solution)/shard_map/pallas_call | solution.py:268
  214.8 13.4 %shard_map.176 = bf16[48,512]{1,0:T(8,128)(2,1)S(1)} custom-call(bf16[768,1024]{1,0:T(8,128)(2,1)S(1)} %copy-done.4, bf16[768,1024]{1,0:T(8,128)(2,1)S(1)} %copy-done.6, bf16[768,1024]{1,0:T(8,128)(2,1)} %collective-permute-done.2.refs_2_, bf16[768,1024]{1,0:T(8,128)(2,1)} %collective-permute-done.4.refs_3_, ...), custom_call_target="tpu_custom_call" | custom-call | flops 6442450944 | bytes 14680064 | tf_op jit(solution)/shard_map/pallas_call | solution.py:116
  228.9 3.4 %all-to-all-start.1 = ((bf16[8,12,512]{2,1,0:T(8,128)(2,1)}), bf16[8,12,512]{2,1,0:T(8,128)(2,1)S(1)}, u32[]{:S(2)}, u32[]{:S(2)}) async-start(bf16[8,12,512]{2,1,0:T(8,128)(2,1)} %bitcast_select_fusion), calls=%async_computation.1 | async-start | bytes 262144 | tf_op jit(solution)/shard_map/all_to_all | solution.py:445
  233.2 4.5 %all-to-all-done.1 = bf16[8,12,512]{2,1,0:T(8,128)(2,1)S(1)} async-done(((bf16[8,12,512]{2,1,0:T(8,128)(2,1)}), bf16[8,12,512]{2,1,0:T(8,128)(2,1)S(1)}, u32[]{:S(2)}, u32[]{:S(2)}) %all-to-all-start.1) | async-done | bytes 98336 | tf_op jit(solution)/shard_map/all_to_all | solution.py:445
  (203 shorter events, 100.9 us)
Async XLA Ops:
  7.2 206.2 %all-gather.3.cloned.1.call-start = ((), (), s32[]{:S(2)}) async-start(), calls=%async_computation.2 | async-start | bytes 9437184 | tf_op jit(solution)/shard_map/all_gather | solution.py:330
  7.9 38.9 %collective-permute-start = (bf16[768,1024]{1,0:T(8,128)(2,1)}, bf16[768,1024]{1,0:T(8,128)(2,1)S(1)}, u32[]{:S(2)}, u32[]{:S(2)}) collective-permute-start(bf16[768,1024]{1,0:T(8,128)(2,1)} %refs_0_.1), channel_id=1, source_target_pairs={{0,1},{1,2},{2,3},{4,5},{5,6},{6,7},{8,9},{9,10},{10,11},{12,13},{... | collective-permute-start | bytes 4718600 | tf_op jit(solution)/shard_map/ppermute | solution.py:143
  13.0 38.1 %collective-permute-start.1 = (bf16[768,1024]{1,0:T(8,128)(2,1)}, bf16[768,1024]{1,0:T(8,128)(2,1)}, u32[]{:S(2)}, u32[]{:S(2)}) collective-permute-start(bf16[768,1024]{1,0:T(8,128)(2,1)} %refs_0_.1), channel_id=1, source_target_pairs={{1,0},{2,1},{3,2},{5,4},{6,5},{7,6},{9,8},{10,9},{11,10},{13,12},{... | collective-permute-start | bytes 4718600 | tf_op jit(solution)/shard_map/ppermute | solution.py:143
  46.8 65.4 %copy-start.5 = (bf16[768,1024]{1,0:T(8,128)(2,1)}, bf16[768,1024]{1,0:T(8,128)(2,1)S(1)}, u32[]{:S(2)}) copy-start(bf16[768,1024]{1,0:T(8,128)(2,1)S(1)} %collective-permute-done.refs_1_) | copy-start | bytes 4718596
  51.0 29.0 %copy-start.8 = (bf16[16,32,512]{2,1,0:T(8,128)(2,1)S(1)}, bf16[16,32,512]{2,1,0:T(8,128)(2,1)}, u32[]{:S(2)}) copy-start(bf16[16,32,512]{2,1,0:T(8,128)(2,1)} %param.29) | copy-start | bytes 1572868
  53.2 34.1 %copy-start.7 = (bf16[16,32,512]{2,1,0:T(8,128)(2,1)S(1)}, bf16[16,32,512]{2,1,0:T(8,128)(2,1)}, u32[]{:S(2)}) copy-start(bf16[16,32,512]{2,1,0:T(8,128)(2,1)} %param.30) | copy-start | bytes 1572868
  93.5 23.4 %all-to-all-start = ((f32[4,48,516]{2,1,0:T(8,128)}), f32[4,48,516]{2,1,0:T(8,128)}, u32[]{:S(2)}, u32[]{:S(2)}) async-start(f32[4,48,516]{2,1,0:T(8,128)} %pad_maximum_fusion.2), calls=%async_computation | async-start | bytes 983040 | tf_op jit(solution)/shard_map/all_to_all | solution.py:389
  108.8 48.5 %collective-permute-start.8 = (bf16[16,32,512]{2,0,1:T(8,128)(2,1)}, bf16[16,32,512]{2,0,1:T(8,128)(2,1)}, u32[]{:S(2)}, u32[]{:S(2)}) collective-permute-start(bf16[16,32,512]{2,0,1:T(8,128)(2,1)} %copy.177), channel_id=1, source_target_pairs={{0,16},{4,20},{8,24},{12,28},{16,0},{20,4},{24,8},{28,12},{1,17},{... | collective-permute-start | bytes 1572872 | tf_op jit(solution)/shard_map/ppermute | solution.py:40
  110.7 48.7 %collective-permute-start.6 = (bf16[16,32,512]{2,0,1:T(8,128)(2,1)}, bf16[16,32,512]{2,0,1:T(8,128)(2,1)}, u32[]{:S(2)}, u32[]{:S(2)}) collective-permute-start(bf16[16,32,512]{2,0,1:T(8,128)(2,1)} %copy.174), channel_id=1, source_target_pairs={{0,8},{4,12},{8,0},{12,4},{16,24},{20,28},{24,16},{28,20},{1,9},{5... | collective-permute-start | bytes 1572872 | tf_op jit(solution)/shard_map/ppermute | solution.py:40
  112.2 41.9 %collective-permute-start.2 = (bf16[768,1024]{1,0:T(8,128)(2,1)S(1)}, bf16[768,1024]{1,0:T(8,128)(2,1)}, u32[]{:S(2)}, u32[]{:S(2)}) collective-permute-start(bf16[768,1024]{1,0:T(8,128)(2,1)S(1)} %collective-permute-done.refs_1_), channel_id=1, source_target_pairs={{1,2},{2,3},{5,6},{6,7},{9,10},{10,11},{13,14},{14,15},{17,18},{18... | collective-permute-start | bytes 4718600 | tf_op jit(solution)/shard_map/ppermute | solution.py:143
  114.1 40.1 %collective-permute-start.3 = (bf16[768,1024]{1,0:T(8,128)(2,1)}, bf16[768,1024]{1,0:T(8,128)(2,1)}, u32[]{:S(2)}, u32[]{:S(2)}) collective-permute-start(bf16[768,1024]{1,0:T(8,128)(2,1)} %collective-permute-done.1.refs_4_), channel_id=1, source_target_pairs={{1,0},{2,1},{5,4},{6,5},{9,8},{10,9},{13,12},{14,13},{17,16},{18,1... | collective-permute-start | bytes 4718600 | tf_op jit(solution)/shard_map/ppermute | solution.py:143
  142.6 19.2 %copy-start.21 = (pred[16]{0:T(512)(128)(4,1)S(1)}, pred[16]{0:T(512)(128)(4,1)}, u32[]{:S(2)}) copy-start(pred[16]{0:T(512)(128)(4,1)} %get-tuple-element.97) | copy-start | bytes 52
  142.6 19.2 %copy-start.22 = (pred[16]{0:T(512)(128)(4,1)S(1)}, pred[16]{0:T(512)(128)(4,1)}, u32[]{:S(2)}) copy-start(pred[16]{0:T(512)(128)(4,1)} %get-tuple-element.98) | copy-start | bytes 52
  142.6 19.2 %copy-start.23 = (pred[16]{0:T(512)(128)(4,1)S(1)}, pred[16]{0:T(512)(128)(4,1)}, u32[]{:S(2)}) copy-start(pred[16]{0:T(512)(128)(4,1)} %get-tuple-element.99) | copy-start | bytes 52
  142.6 27.9 %copy-start.26 = (pred[16]{0:T(512)(128)(4,1)S(1)}, pred[16]{0:T(512)(128)(4,1)}, u32[]{:S(2)}) copy-start(pred[16]{0:T(512)(128)(4,1)} %get-tuple-element.109) | copy-start | bytes 52
  142.6 27.9 %copy-start.27 = (pred[16]{0:T(512)(128)(4,1)S(1)}, pred[16]{0:T(512)(128)(4,1)}, u32[]{:S(2)}) copy-start(pred[16]{0:T(512)(128)(4,1)} %get-tuple-element.95) | copy-start | bytes 52
  145.8 27.1 %copy-start.24 = (pred[16]{0:T(512)(128)(4,1)S(1)}, pred[16]{0:T(512)(128)(4,1)}, u32[]{:S(2)}) copy-start(pred[16]{0:T(512)(128)(4,1)} %get-tuple-element.110) | copy-start | bytes 52
  145.9 27.1 %copy-start.25 = (pred[16]{0:T(512)(128)(4,1)S(1)}, pred[16]{0:T(512)(128)(4,1)}, u32[]{:S(2)}) copy-start(pred[16]{0:T(512)(128)(4,1)} %get-tuple-element.111) | copy-start | bytes 52
  154.2 59.2 %collective-permute-start.4 = (bf16[768,1024]{1,0:T(8,128)(2,1)}, bf16[768,1024]{1,0:T(8,128)(2,1)}, u32[]{:S(2)}, u32[]{:S(2)}) collective-permute-start(bf16[768,1024]{1,0:T(8,128)(2,1)} %collective-permute-done.2.refs_2_), channel_id=1, source_target_pairs={{2,3},{6,7},{10,11},{14,15},{18,19},{22,23},{26,27},{30,31}} | collective-permute-start | bytes 4718600 | tf_op jit(solution)/shard_map/ppermute | solution.py:143
  156.0 57.4 %collective-permute-start.5 = (bf16[768,1024]{1,0:T(8,128)(2,1)}, bf16[768,1024]{1,0:T(8,128)(2,1)}, u32[]{:S(2)}, u32[]{:S(2)}) collective-permute-start(bf16[768,1024]{1,0:T(8,128)(2,1)} %collective-permute-done.3.refs_5_), channel_id=1, source_target_pairs={{1,0},{5,4},{9,8},{13,12},{17,16},{21,20},{25,24},{29,28}} | collective-permute-start | bytes 4718600 | tf_op jit(solution)/shard_map/ppermute | solution.py:143
  158.8 11.7 %collective-permute-start.9 = (bf16[16,32,512]{2,0,1:T(8,128)(2,1)S(1)}, bf16[16,32,512]{2,0,1:T(8,128)(2,1)S(1)}, u32[]{:S(2)}, u32[]{:S(2)}) collective-permute-start(bf16[16,32,512]{2,0,1:T(8,128)(2,1)S(1)} %broadcast_select_fusion), channel_id=1, source_target_pairs={{0,8},{4,12},{8,0},{12,4},{16,24},{20,28},{24,16},{28,20},{1,9},{5... | collective-permute-start | bytes 1572872 | tf_op jit(solution)/shard_map/ppermute | solution.py:40
  161.3 11.7 %collective-permute-start.7 = (bf16[16,32,512]{2,0,1:T(8,128)(2,1)S(1)}, bf16[16,32,512]{2,0,1:T(8,128)(2,1)S(1)}, u32[]{:S(2)}, u32[]{:S(2)}) collective-permute-start(bf16[16,32,512]{2,0,1:T(8,128)(2,1)S(1)} %broadcast_select_fusion.1), channel_id=1, source_target_pairs={{0,16},{4,20},{8,24},{12,28},{16,0},{20,4},{24,8},{28,12},{1,17},{... | collective-permute-start | bytes 1572872 | tf_op jit(solution)/shard_map/ppermute | solution.py:40
  175.2 38.2 %copy-start.4 = (bf16[768,1024]{1,0:T(8,128)(2,1)S(1)}, bf16[768,1024]{1,0:T(8,128)(2,1)}, u32[]{:S(2)}) copy-start(bf16[768,1024]{1,0:T(8,128)(2,1)} %refs_0_.1) | copy-start | bytes 4718596
  228.9 8.8 %all-to-all-start.1 = ((bf16[8,12,512]{2,1,0:T(8,128)(2,1)}), bf16[8,12,512]{2,1,0:T(8,128)(2,1)S(1)}, u32[]{:S(2)}, u32[]{:S(2)}) async-start(bf16[8,12,512]{2,1,0:T(8,128)(2,1)} %bitcast_select_fusion), calls=%async_computation.1 | async-start | bytes 262144 | tf_op jit(solution)/shard_map/all_to_all | solution.py:445
  (18 other events, 224.5 us)
Sparse Core Ops, SparseCore 0:
  9.9 58.6 all-gather.2

commit v4 on v3

--- a/solution.py
+++ b/solution.py
@@ -344,12 +344,7 @@
     every = lax.all_gather(
         jnp.concatenate(made, axis=1), "hyp", axis=0, tiled=False, axis_index_groups=beam_groups
     )
-    every, hops[0], late_keys, late_values = lax.optimization_barrier(
-        (every, hops[0], past_keys, past_values)
-    )
     every = every.reshape(BEAMS, STEPS, rows, 3, head_width)
-    for step in range(2, max(head_parts - 1, 2)):
-        hops.append(travel(hops[-1], step))
     queries, keys, values = every[:, :, :, 0], every[:, :, :, 1], every[:, :, :, 2]
 
     parent_view = parents.reshape(STEPS, BEAMS, -1)
@@ -386,6 +381,11 @@
         ],
         axis=2,
     )
+    packed, hops[0], late_keys, late_values = lax.optimization_barrier(
+        (packed, hops[0], past_keys, past_values)
+    )
+    for step in range(2, max(head_parts - 1, 2)):
+        hops.append(travel(hops[-1], step))
     returned = lax.all_to_all(
         packed, "hyp", 0, 0, tiled=True, axis_index_groups=beam_groups
     ).reshape(BEAMS, STEPS, rows, head_width + heads * 2)

time: 248 us -> 244 us (0.984)
  waiting for transfers between devices: 22.1 us -> 12.8 us
  local copies, waits for them, and re-layouts: 76.5 us -> 80.1 us
    ppermute x3, waiting for transfers between devices: 3.84 us -> 0.01 us  [travel(): lax.ppermute(up, 'head', upward)]
    ppermute x3, waiting for transfers between devices: 4.22 us -> 0.86 us  [travel(): lax.ppermute(down, 'head', downward)]
    select_n x4, other arithmetic: 2.46 us -> 5.17 us  [pick(): jnp.where((selector == position).reshape(shape), candidates[position], ch...]
    unnamed x73 -> x87, local copies, waits for them, and re-layouts: 5.01 us -> 6.71 us
  transfers between devices with their start and end apart: 13 -> 13, of which waited for: 5 -> 4; matrix products, arithmetic and copies ran while one was open for 46% -> 48% of each run, Pallas kernels for 15% -> 15%
where the time goes in v4:
time: 244 us; the launch traced here: 241 us
  local copies, waits for them, and re-layouts  80.1 us (33%)
  Pallas kernels  48.9 us (20%)
  other arithmetic  34.1 us (14%)
  starting transfers between devices  24.5 us (10%)
  blocking collectives  16.4 us (7%)
  between operations  15.6 us (6%)
  waiting for transfers between devices  12.8 us (5%)
  matrix products  8.77 us (4%)
    pallas_call x1, Pallas kernels, cross_queries(): pl.pallas_call(functools.partial(cross_query_kernel, docs_here), out_shap...  35.6 us
    all_gather x1, blocking collectives, shards(): lax.all_gather(jnp.concatenate(made, axis=1), 'hyp', axis=0, tiled=False,...  16.4 us
    pallas_call x1, Pallas kernels, document_attend(): pl.pallas_call(functools.partial(document_kernel, size), out_shape=jax.Sh...  13.3 us
    ppermute x3, starting transfers between devices, travel(): lax.ppermute(up, 'head', upward)  8.71 us
    exp x6, local copies, waits for them, and re-layouts, shards(): weight = jnp.exp(score - top)  7.87 us
    reduce_sum x6, local copies, waits for them, and re-layouts, shards(): score_list.append(jnp.sum(my_query * key, axis=-1) * scaling)  7.29 us
    unnamed x87, local copies, waits for them, and re-layouts  6.71 us
    ppermute x4, waiting for transfers between devices, swap(): return lax.ppermute(block, 'hyp', route)  6.69 us
  transfers between devices with their start and end apart: 13, of which 4 were waited for; matrix products, arithmetic and copies ran while one was open for 48% of the time, Pallas kernels for 15%

profile of v4, /device:TPU:0, one launch (start us, length us, event | category | flops | bytes accessed | tf_op | source)
XLA Modules:
  0.0 241.2 jit_solution(10472282065027346645)
XLA Ops:
  7.9 5.0 %collective-permute-start = (bf16[768,1024]{1,0:T(8,128)(2,1)}, bf16[768,1024]{1,0:T(8,128)(2,1)S(1)}, u32[]{:S(2)}, u32[]{:S(2)}) collective-permute-start(bf16[768,1024]{1,0:T(8,128)(2,1)} %refs_0_.1), channel_id=1, source_target_pairs={{0,1},{1,2},{2,3},{4,5},{5,6},{6,7},{8,9},{9,10},{10,11},{12,13},{... | collective-permute-start | bytes 4718600 | tf_op jit(solution)/shard_map/ppermute | solution.py:143
  17.8 3.8 %convolution_convert_fusion = bf16[48,512]{1,0:T(8,128)(2,1)S(1)} fusion(bf16[48,4096]{1,0:T(8,128)(2,1)S(1)} %multiply_convert_fusion, bf16[4096,512]{1,0:T(8,128)(2,1)} %param.22), kind=kOutput, calls=%fused_computation.2 | convolution fusion | flops 201351168 | bytes 4636672 | tf_op jit(solution)/shard_map/dot_general | solution.py:341
  23.4 16.4 %all-gather = bf16[192,1536]{1,0:T(8,128)(2,1)} all-gather(bf16[48,1536]{1,0:T(8,128)(2,1)S(1)} %pad_maximum_fusion.3), channel_id=2, replica_groups={{0,8,16,24},{4,12,20,28},{1,9,17,25},{5,13,21,29},{2,10,18,26},{6,14,22..., dimensions={0}, use_global_device_ids=true | all-gather | bytes 737280 | tf_op jit(solution)/shard_map/all_gather | solution.py:344
  39.8 2.2 reshape.1084
  41.9 3.8 %fusion.50 = (bf16[4,3,16,1,512]{4,3,2,1,0:T(2,128)(2,1)}, bf16[4,3,16,1,512]{4,3,2,1,0:T(2,128)(2,1)}, bf16[4,3,16,1,512]{4,3,2,1,0:T(2,128)(2,1)S(1)}) fusion(bf16[4,3,16,3,512]{4,3,2,1,0:T(4,128)(2,1)} %reshape.1084), kind=kLoop, calls=%fused_computation.170 | loop fusion | bytes 1179648 | tf_op jit(solution)/shard_map/slice | solution.py:348
  47.8 1.9 copy_bitcast_fusion
  61.0 1.7 reshape_squeeze.3
  69.4 1.6 multiply_reduce_fusion.2
  71.0 1.7 multiply_reduce_fusion.5
  72.8 1.9 fusion.57
  87.3 2.1 reshape.1087
  92.2 1.9 pad_maximum_fusion.2
  97.2 4.2 %all-to-all-start = ((f32[4,48,516]{2,1,0:T(8,128)}), f32[4,48,516]{2,1,0:T(8,128)}, u32[]{:S(2)}, u32[]{:S(2)}) async-start(f32[4,48,516]{2,1,0:T(8,128)} %pad_maximum_fusion.2), calls=%async_computation | async-start | bytes 983040 | tf_op jit(solution)/shard_map/all_to_all | solution.py:389
  101.9 1.6 fusion.52
  105.7 2.0 collective-permute-start.8
  109.1 1.9 collective-permute-start.2
  150.2 1.8 collective-permute-start.4
  156.1 2.2 broadcast_select_fusion.1
  160.7 5.6 %collective-permute-done.9 = bf16[16,32,512]{2,0,1:T(8,128)(2,1)S(1)} collective-permute-done((bf16[16,32,512]{2,0,1:T(8,128)(2,1)S(1)}, bf16[16,32,512]{2,0,1:T(8,128)(2,1)S(1)}, u32[]{:S(2)}, u32[]{:S(2)}) %collective-permute-start.9) | collective-permute-done | bytes 524320 | tf_op jit(solution)/shard_map/ppermute | solution.py:40
  171.3 2.2 copy-done.2
  173.5 35.6 %shard_map.175 = bf16[4,48,512]{2,1,0:T(8,128)(2,1)S(1)} custom-call(bf16[48,512]{1,0:T(8,128)(2,1)S(1)} %pad_maximum_fusion.4.context, bf16[512,4096]{1,0:T(8,128)(2,1)S(1)} %copy-done.1, f32[48,4096]{1,0:T(8,128)S(1)} %bitcast.307, f32[1,4096]{1,0:T(1,128)S(1)} %bitcast.308, bf16[4096,512]{1,0:T(8,128)(2,1)S(1)} %copy-done.2), custom_call_target="tpu_custom_call" | custom-call | flops 402653184 | bytes 33554432 | tf_op jit(solution)/shard_map/pallas_call | solution.py:268
  210.7 13.3 %shard_map.176 = bf16[48,512]{1,0:T(8,128)(2,1)S(1)} custom-call(bf16[768,1024]{1,0:T(8,128)(2,1)S(1)} %copy-done.4, bf16[768,1024]{1,0:T(8,128)(2,1)S(1)} %copy-done.6, bf16[768,1024]{1,0:T(8,128)(2,1)} %collective-permute-done.2.refs_2_, bf16[768,1024]{1,0:T(8,128)(2,1)} %collective-permute-done.4.refs_3_, ...), custom_call_target="tpu_custom_call" | custom-call | flops 6442450944 | bytes 14680064 | tf_op jit(solution)/shard_map/pallas_call | solution.py:116
  224.8 3.4 %all-to-all-start.1 = ((bf16[8,12,512]{2,1,0:T(8,128)(2,1)}), bf16[8,12,512]{2,1,0:T(8,128)(2,1)S(1)}, u32[]{:S(2)}, u32[]{:S(2)}) async-start(bf16[8,12,512]{2,1,0:T(8,128)(2,1)} %bitcast_select_fusion), calls=%async_computation.1 | async-start | bytes 262144 | tf_op jit(solution)/shard_map/all_to_all | solution.py:445
  229.1 4.5 %all-to-all-done.1 = bf16[8,12,512]{2,1,0:T(8,128)(2,1)S(1)} async-done(((bf16[8,12,512]{2,1,0:T(8,128)(2,1)}), bf16[8,12,512]{2,1,0:T(8,128)(2,1)S(1)}, u32[]{:S(2)}, u32[]{:S(2)}) %all-to-all-start.1) | async-done | bytes 98336 | tf_op jit(solution)/shard_map/all_to_all | solution.py:445
  (217 shorter events, 103.7 us)
Async XLA Ops:
  7.2 202.1 %all-gather.3.cloned.1.call-start = ((), (), s32[]{:S(2)}) async-start(), calls=%async_computation.2 | async-start | bytes 9437184 | tf_op jit(solution)/shard_map/all_gather | solution.py:330
  7.9 89.3 %collective-permute-start = (bf16[768,1024]{1,0:T(8,128)(2,1)}, bf16[768,1024]{1,0:T(8,128)(2,1)S(1)}, u32[]{:S(2)}, u32[]{:S(2)}) collective-permute-start(bf16[768,1024]{1,0:T(8,128)(2,1)} %refs_0_.1), channel_id=1, source_target_pairs={{0,1},{1,2},{2,3},{4,5},{5,6},{6,7},{8,9},{9,10},{10,11},{12,13},{... | collective-permute-start | bytes 4718600 | tf_op jit(solution)/shard_map/ppermute | solution.py:143
  13.0 84.2 %collective-permute-start.1 = (bf16[768,1024]{1,0:T(8,128)(2,1)}, bf16[768,1024]{1,0:T(8,128)(2,1)}, u32[]{:S(2)}, u32[]{:S(2)}) collective-permute-start(bf16[768,1024]{1,0:T(8,128)(2,1)} %refs_0_.1), channel_id=1, source_target_pairs={{1,0},{2,1},{3,2},{5,4},{6,5},{7,6},{9,8},{10,9},{11,10},{13,12},{... | collective-permute-start | bytes 4718600 | tf_op jit(solution)/shard_map/ppermute | solution.py:143
  22.6 24.6 %copy-start.34 = (s32[3,128]{1,0:T(4,128)S(1)}, s32[3,128]{1,0:T(4,128)}, u32[]{:S(2)}) copy-start(s32[3,128]{1,0:T(4,128)} %param.31) | copy-start | bytes 4612
  39.8 33.0 %copy-start.8 = (bf16[16,32,512]{2,1,0:T(8,128)(2,1)S(1)}, bf16[16,32,512]{2,1,0:T(8,128)(2,1)}, u32[]{:S(2)}) copy-start(bf16[16,32,512]{2,1,0:T(8,128)(2,1)} %param.29) | copy-start | bytes 1572868
  41.9 43.1 %copy-start.7 = (bf16[16,32,512]{2,1,0:T(8,128)(2,1)S(1)}, bf16[16,32,512]{2,1,0:T(8,128)(2,1)}, u32[]{:S(2)}) copy-start(bf16[16,32,512]{2,1,0:T(8,128)(2,1)} %param.30) | copy-start | bytes 1572868
  97.2 56.2 %copy-start.5 = (bf16[768,1024]{1,0:T(8,128)(2,1)}, bf16[768,1024]{1,0:T(8,128)(2,1)S(1)}, u32[]{:S(2)}) copy-start(bf16[768,1024]{1,0:T(8,128)(2,1)S(1)} %collective-permute-done.refs_1_) | copy-start | bytes 4718596
  97.2 15.1 %all-to-all-start = ((f32[4,48,516]{2,1,0:T(8,128)}), f32[4,48,516]{2,1,0:T(8,128)}, u32[]{:S(2)}, u32[]{:S(2)}) async-start(f32[4,48,516]{2,1,0:T(8,128)} %pad_maximum_fusion.2), calls=%async_computation | async-start | bytes 983040 | tf_op jit(solution)/shard_map/all_to_all | solution.py:389
  103.5 45.8 %copy-start.13 = (bf16[4,1,16,512]{3,2,1,0:T(8,128)(2,1)}, bf16[4,1,16,512]{3,2,1,0:T(8,128)(2,1)S(1)}, u32[]{:S(2)}) copy-start(bf16[4,1,16,512]{3,2,1,0:T(8,128)(2,1)S(1)} %get-tuple-element.57) | copy-start | bytes 196612
  105.7 47.7 %collective-permute-start.8 = (bf16[16,32,512]{2,0,1:T(8,128)(2,1)}, bf16[16,32,512]{2,0,1:T(8,128)(2,1)}, u32[]{:S(2)}, u32[]{:S(2)}) collective-permute-start(bf16[16,32,512]{2,0,1:T(8,128)(2,1)} %copy.177), channel_id=1, source_target_pairs={{0,16},{4,20},{8,24},{12,28},{16,0},{20,4},{24,8},{28,12},{1,17},{... | collective-permute-start | bytes 1572872 | tf_op jit(solution)/shard_map/ppermute | solution.py:40
  107.6 48.4 %collective-permute-start.6 = (bf16[16,32,512]{2,0,1:T(8,128)(2,1)}, bf16[16,32,512]{2,0,1:T(8,128)(2,1)}, u32[]{:S(2)}, u32[]{:S(2)}) collective-permute-start(bf16[16,32,512]{2,0,1:T(8,128)(2,1)} %copy.174), channel_id=1, source_target_pairs={{0,8},{4,12},{8,0},{12,4},{16,24},{20,28},{24,16},{28,20},{1,9},{5... | collective-permute-start | bytes 1572872 | tf_op jit(solution)/shard_map/ppermute | solution.py:40
  109.1 40.3 %collective-permute-start.2 = (bf16[768,1024]{1,0:T(8,128)(2,1)S(1)}, bf16[768,1024]{1,0:T(8,128)(2,1)}, u32[]{:S(2)}, u32[]{:S(2)}) collective-permute-start(bf16[768,1024]{1,0:T(8,128)(2,1)S(1)} %collective-permute-done.refs_1_), channel_id=1, source_target_pairs={{1,2},{2,3},{5,6},{6,7},{9,10},{10,11},{13,14},{14,15},{17,18},{18... | collective-permute-start | bytes 4718600 | tf_op jit(solution)/shard_map/ppermute | solution.py:143
  111.0 39.2 %collective-permute-start.3 = (bf16[768,1024]{1,0:T(8,128)(2,1)}, bf16[768,1024]{1,0:T(8,128)(2,1)}, u32[]{:S(2)}, u32[]{:S(2)}) collective-permute-start(bf16[768,1024]{1,0:T(8,128)(2,1)} %collective-permute-done.1.refs_4_), channel_id=1, source_target_pairs={{1,0},{2,1},{5,4},{6,5},{9,8},{10,9},{13,12},{14,13},{17,16},{18,1... | collective-permute-start | bytes 4718600 | tf_op jit(solution)/shard_map/ppermute | solution.py:143
  149.4 18.3 %copy-start.16 = (bf16[16,1,512]{2,0,1:T(8,128)(2,1)S(1)}, bf16[16,1,512]{2,0,1:T(8,128)(2,1)}, u32[]{:S(2)}) copy-start(bf16[16,1,512]{2,0,1:T(8,128)(2,1)} %get-tuple-element.51) | copy-start | bytes 49156
  150.2 59.0 %collective-permute-start.4 = (bf16[768,1024]{1,0:T(8,128)(2,1)}, bf16[768,1024]{1,0:T(8,128)(2,1)}, u32[]{:S(2)}, u32[]{:S(2)}) collective-permute-start(bf16[768,1024]{1,0:T(8,128)(2,1)} %collective-permute-done.2.refs_2_), channel_id=1, source_target_pairs={{2,3},{6,7},{10,11},{14,15},{18,19},{22,23},{26,27},{30,31}} | collective-permute-start | bytes 4718600 | tf_op jit(solution)/shard_map/ppermute | solution.py:143
  152.0 57.2 %collective-permute-start.5 = (bf16[768,1024]{1,0:T(8,128)(2,1)}, bf16[768,1024]{1,0:T(8,128)(2,1)}, u32[]{:S(2)}, u32[]{:S(2)}) collective-permute-start(bf16[768,1024]{1,0:T(8,128)(2,1)} %collective-permute-done.3.refs_5_), channel_id=1, source_target_pairs={{1,0},{5,4},{9,8},{13,12},{17,16},{21,20},{25,24},{29,28}} | collective-permute-start | bytes 4718600 | tf_op jit(solution)/shard_map/ppermute | solution.py:143
  153.4 17.9 %copy-start.3 = (f32[4096]{0:T(1024)S(1)}, f32[4096]{0:T(1024)}, u32[]{:S(2)}) copy-start(f32[4096]{0:T(1024)} %param.24) | copy-start | bytes 49156
  154.8 11.5 %collective-permute-start.9 = (bf16[16,32,512]{2,0,1:T(8,128)(2,1)S(1)}, bf16[16,32,512]{2,0,1:T(8,128)(2,1)S(1)}, u32[]{:S(2)}, u32[]{:S(2)}) collective-permute-start(bf16[16,32,512]{2,0,1:T(8,128)(2,1)S(1)} %broadcast_select_fusion), channel_id=1, source_target_pairs={{0,8},{4,12},{8,0},{12,4},{16,24},{20,28},{24,16},{28,20},{1,9},{5... | collective-permute-start | bytes 1572872 | tf_op jit(solution)/shard_map/ppermute | solution.py:40
  158.2 11.5 %collective-permute-start.7 = (bf16[16,32,512]{2,0,1:T(8,128)(2,1)}, bf16[16,32,512]{2,0,1:T(8,128)(2,1)}, u32[]{:S(2)}, u32[]{:S(2)}) collective-permute-start(bf16[16,32,512]{2,0,1:T(8,128)(2,1)} %broadcast_select_fusion.1), channel_id=1, source_target_pairs={{0,16},{4,20},{8,24},{12,28},{16,0},{20,4},{24,8},{28,12},{1,17},{... | collective-permute-start | bytes 1572872 | tf_op jit(solution)/shard_map/ppermute | solution.py:40
  173.5 35.8 %copy-start.4 = (bf16[768,1024]{1,0:T(8,128)(2,1)S(1)}, bf16[768,1024]{1,0:T(8,128)(2,1)}, u32[]{:S(2)}) copy-start(bf16[768,1024]{1,0:T(8,128)(2,1)} %refs_0_.1) | copy-start | bytes 4718596
  209.2 14.9 %copy-start.35 = (pred[8]{0:T(512)(128)(4,1)S(1)}, pred[8]{0:T(512)(128)(4,1)}, u32[]{:S(2)}) copy-start(pred[8]{0:T(512)(128)(4,1)} %broadcast_in_dim.272) | copy-start | bytes 28
  209.2 19.0 %copy-start.14 = (bf16[16,1,512]{2,0,1:T(8,128)(2,1)S(1)}, bf16[16,1,512]{2,0,1:T(8,128)(2,1)}, u32[]{:S(2)}) copy-start(bf16[16,1,512]{2,0,1:T(8,128)(2,1)} %get-tuple-element.74) | copy-start | bytes 49156
  209.2 19.0 %copy-start.15 = (bf16[16,1,512]{2,0,1:T(8,128)(2,1)S(1)}, bf16[16,1,512]{2,0,1:T(8,128)(2,1)}, u32[]{:S(2)}) copy-start(bf16[16,1,512]{2,0,1:T(8,128)(2,1)} %get-tuple-element.54) | copy-start | bytes 49156
  224.8 8.8 %all-to-all-start.1 = ((bf16[8,12,512]{2,1,0:T(8,128)(2,1)}), bf16[8,12,512]{2,1,0:T(8,128)(2,1)S(1)}, u32[]{:S(2)}, u32[]{:S(2)}) async-start(bf16[8,12,512]{2,1,0:T(8,128)(2,1)} %bitcast_select_fusion), calls=%async_computation.1 | async-start | bytes 262144 | tf_op jit(solution)/shard_map/all_to_all | solution.py:445
  (25 other events, 156.2 us)
Sparse Core Ops, SparseCore 0:
  9.9 60.2 all-gather.2
